TPU v7x, 128 devices: a whole 4x4x4 slice. The times are simulated.
128 devices in a mesh: replica: 8 (over y_lo, z), fsdp: 16 (over x, y_hi, core).
Axes of the slice: x: 4, y: 4 (y_hi: 2, y_lo: 2; y = y_hi * 2 + y_lo), z: 4, core: 2. Of those that a mesh axis runs over, the one named last changes fastest.
Arguments:
- hidden_states: bfloat16 [32768, 8192], P(('replica', 'fsdp')), may hold values from -24 to 24
- key_weight: bfloat16 [8192, 1024], P('fsdp'), may hold values from -0.13258252 to 0.13258252
- previous_peak: float32 [1], replicated, may hold values from 0.088388346 to 0.12705825
- key_cotangent: bfloat16 [32768, 1024], P(('replica', 'fsdp')), may hold values from -6 to 6
Outputs:
- projected_keys: bfloat16 [32768, 1024], P(('replica', 'fsdp'))
- input_gradient: bfloat16 [32768, 8192], P(('replica', 'fsdp'))
- weight_gradient: bfloat16 [8192, 1024], P('fsdp')
- peak_ratio: float32 [1], replicated
All inputs are finite; a program needn't handle non-finite values.
Results may differ from a plain program's by a relative error of at most 0.025.
Values may be sent and summed in bfloat16 or wider, within the bound.
A program may use at most 128 MiB of HBM per device.

v0:
```python
import jax
import jax.numpy as jnp
from jax import lax
from jax.sharding import PartitionSpec as P


def quantize(weight, limit):
    return jnp.clip(weight.astype(jnp.float32) * (448.0 / limit), -448.0, 448.0).astype(
        jnp.bfloat16
    )


def body(hidden_states, key_weight, previous_peak, key_cotangent):
    limit = previous_peak[0]
    unscale = limit / 448.0
    tok_rows = hidden_states.shape[0]
    source = quantize(key_weight, limit)
    local_peak = jnp.max(jnp.abs(key_weight.astype(jnp.float32)))
    peak = lax.pmax(local_peak, "fsdp")
    gathered = lax.all_gather(source, "fsdp", axis=0, tiled=True)
    keys_sum = jnp.dot(hidden_states, gathered, preferred_element_type=jnp.float32)
    grad_sum = lax.dot_general(
        key_cotangent, gathered, (((1,), (1,)), ((), ())), preferred_element_type=jnp.float32
    )
    projected_keys = (keys_sum * unscale).astype(jnp.bfloat16)
    input_gradient = (grad_sum * unscale).astype(jnp.bfloat16)
    group = lax.psum_scatter(
        lax.dot_general(
            hidden_states,
            key_cotangent,
            (((0,), (0,)), ((), ())),
            preferred_element_type=jnp.float32,
        ).astype(jnp.bfloat16),
        "fsdp",
        scatter_dimension=0,
        tiled=True,
    ).astype(jnp.float32)
    group = group.astype(jnp.bfloat16)
    total = lax.psum(group, "replica").astype(jnp.float32)
    token_count = tok_rows * lax.axis_size("replica") * lax.axis_size("fsdp")
    weight_gradient = (total * token_count ** (-0.5)).astype(jnp.bfloat16)
    peak_ratio = (peak / limit).reshape(1)
    return (projected_keys, input_gradient, weight_gradient, peak_ratio)


def solution(mesh):
    in_specs = (P(("replica", "fsdp"), None), P("fsdp", None), P(), P(("replica", "fsdp"), None))
    out_specs = (P(("replica", "fsdp"), None), P(("replica", "fsdp"), None), P("fsdp", None), P())
    return jax.shard_map(body, mesh=mesh, in_specs=in_specs, out_specs=out_specs, check_vma=False)
```

profile of v0, /device:TPU:0, one launch (start us, length us, event | category | flops | bytes accessed | tf_op | source)
XLA Modules:
  0.0 398.3 jit_solution(9890249715255304401)
XLA Ops:
  7.2 0.0 copy-start
  7.2 0.0 reduce-scatter.2.cloned.1.call-start
  7.2 1.0 copy-done
  8.2 10.5 %convolution_convert_fusion = bf16[8192,1024]{1,0:T(8,128)(2,1)} fusion(bf16[256,8192]{1,0:T(8,128)(2,1)} %param.4, bf16[256,1024]{1,0:T(8,128)(2,1)S(1)} %copy-done), kind=kOutput, calls=%fused_computation | convolution fusion | flops 4303355904 | bytes 21495808 | tf_op jit(solution)/shard_map/dot_general | solution.py:28
  18.7 0.0 copy-start.1
  18.7 0.0 reduce-scatter.2.cloned.1.call-update
  18.7 0.0 all-reduce.2.cloned.1.call-start
  18.8 149.8 %reduce-scatter.2.cloned.1.call-done = bf16[512,1024]{1,0:T(8,128)(2,1)} async-done(((bf16[8192,1024]{1,0:T(8,128)(2,1)}), bf16[512,1024]{1,0:T(8,128)(2,1)}) %reduce-scatter.2.cloned.1.call-update) | async-done | bytes 1048592 | tf_op jit(solution)/shard_map/reduce_scatter | solution.py:27
  168.6 0.0 all-reduce.2.cloned.1.call-update
  168.6 0.0 all-gather.2.cloned.1.call-start
  169.3 0.0 copy-done.1
  169.4 1.9 fusion.4
  171.2 0.0 all-gather.2.cloned.1.call-update
  171.2 34.0 %pmax.7 = f32[]{:T(128)} all-reduce(f32[]{:T(128)} %get-tuple-element.8), channel_id=1, replica_groups=mesh['replica'=8,'fsdp'=16] {'fsdp'}, use_global_device_ids=true, to_apply=%region_3.4 | all-reduce | flops 1 | bytes 8 | tf_op jit(solution)/shard_map/pmax | solution.py:19
  205.9 40.6 %all-reduce.2.cloned.1.call-done = bf16[512,1024]{1,0:T(8,128)(2,1)} async-done(((bf16[512,1024]{1,0:T(8,128)(2,1)}), bf16[512,1024]{1,0:T(8,128)(2,1)}) %all-reduce.2.cloned.1.call-update) | async-done | bytes 1048592 | tf_op jit(solution)/shard_map/psum | solution.py:39
  246.6 2.4 multiply_convert_fusion
  249.0 110.5 %all-gather.2.cloned.1.call-done = bf16[8192,1024]{1,0:T(8,128)(2,1)} async-done(((bf16[512,1024]{1,0:T(8,128)(2,1)}), bf16[8192,1024]{1,0:T(8,128)(2,1)}) %all-gather.2.cloned.1.call-update) | async-done | bytes 16777232 | tf_op jit(solution)/shard_map/all_gather | solution.py:20
  359.5 12.3 %fusion.1 = bf16[256,8192]{0,1:T(8,128)(2,1)} fusion(bf16[8192,1024]{1,0:T(8,128)(2,1)} %all-gather.2.cloned.1.call-done, bf16[256,1024]{1,0:T(8,128)(2,1)S(1)} %copy-done, f32[]{:T(128)S(6)} %div.10), kind=kOutput, calls=%fused_computation.3 | convolution fusion | flops 4299161600 | bytes 21495812 | tf_op jit(solution)/shard_map/dot_general | solution.py:22
  371.8 6.3 %copy.9 = bf16[256,8192]{1,0:T(8,128)(2,1)} copy(bf16[256,8192]{0,1:T(8,128)(2,1)} %fusion.1) | data formatting | bytes 8388608
  378.1 11.5 %fusion.6 = bf16[256,1024]{0,1:T(8,128)(2,1)S(1)} fusion(bf16[8192,1024]{1,0:T(8,128)(2,1)} %all-gather.2.cloned.1.call-done, bf16[256,8192]{1,0:T(8,128)(2,1)} %param.4, f32[]{:T(128)S(6)} %div.10), kind=kOutput, calls=%fused_computation.12 | convolution fusion | flops 4295491584 | bytes 21495812 | tf_op jit(solution)/shard_map/dot_general | solution.py:21
  389.6 1.0 copy.8
Async XLA Ops:
  7.2 1.0 copy-start
  7.2 161.4 %reduce-scatter.2.cloned.1.call-start = ((), (), s32[]{:S(2)}) async-start(), calls=%async_computation.2 | async-start | bytes 17825792 | tf_op jit(solution)/shard_map/reduce_scatter | solution.py:27
  18.7 150.7 %copy-start.1 = (bf16[512,1024]{1,0:T(8,128)(2,1)S(1)}, bf16[512,1024]{1,0:T(8,128)(2,1)}, u32[]{:S(2)}) copy-start(bf16[512,1024]{1,0:T(8,128)(2,1)} %param.5) | copy-start | bytes 3145732
  18.7 227.9 %all-reduce.2.cloned.1.call-start = ((), (), s32[]{:S(2)}) async-start(), calls=%async_computation.3 | async-start | bytes 2097152 | tf_op jit(solution)/shard_map/psum | solution.py:39
  168.6 190.9 %all-gather.2.cloned.1.call-start = ((), (), s32[]{:S(2)}) async-start(), calls=%async_computation.1 | async-start | bytes 17825792 | tf_op jit(solution)/shard_map/all_gather | solution.py:20
Sparse Core Ops, SparseCore 0:
  18.8 149.7 reduce-scatter.1
  171.2 75.2 all-reduce.1
  249.8 109.6 all-gather.1
where the time goes:
time: 400 us; the launch traced here: 398 us
  waiting for transfers between devices  301 us (75%)
  matrix products  34.3 us (9%)
  blocking collectives  34 us (8%)
  between operations  16.2 us (4%)
  local copies, waits for them, and re-layouts  8.31 us (2%)
  other arithmetic  4.27 us (1%)
    reduce_scatter x1, waiting for transfers between devices, body(): lax.psum_scatter(lax.dot_general(hidden_states, key_cotangent, (((0,), (0...  150 us
    all_gather x1, waiting for transfers between devices, body(): gathered = lax.all_gather(source, 'fsdp', axis=0, tiled=True)  111 us
    psum x1, waiting for transfers between devices, body(): total = lax.psum(group, 'replica').astype(jnp.float32)  40.6 us
    pmax x1, blocking collectives, body(): peak = lax.pmax(local_peak, 'fsdp')  34 us
    dot_general x1, matrix products, body(): lax.dot_general(key_cotangent, gathered, (((1,), (1,)), ((), ())), prefer...  12.3 us
    dot_general x1, matrix products, body(): jnp.dot(hidden_states, gathered, preferred_element_type=jnp.float32)  11.5 us
    dot_general x1, matrix products, body(): lax.dot_general(hidden_states, key_cotangent, (((0,), (0,)), ((), ())), p...  10.5 us
    unnamed x6, local copies, waits for them, and re-layouts  8.31 us
  transfers between devices with their start and end apart: 3, of which 3 were waited for; matrix products, arithmetic and copies ran while one was open for 1% of the time, Pallas kernels for 0%

commit v1 on v0

v1 whole, which is shorter than its diff:
```python
import functools

import jax
import jax.numpy as jnp
from jax import lax
from jax.experimental import pallas as pl
from jax.experimental.pallas import tpu as pltpu
from jax.sharding import PartitionSpec as P

MESH = pl.DeviceIdType.MESH
AXES = ("x", "y", "z")
GATHER = ((0, 384, ("y", "z", "x")), (384, 384, ("z", "x", "y")), (768, 256, ("x", "y", "z")))
REDUCE = ((0, 384, ("x", "z", "y")), (384, 256, ("y", "x", "z")), (640, 384, ("z", "y", "x")))
ROWS = 64
WIDTH = 1024
TOK = 256
SLOTS = 8
BLOCK = 512


def position():
    replica, fsdp = lax.axis_index("replica"), lax.axis_index("fsdp")
    y_lo, z = replica // 4, lax.rem(replica, 4)
    x, y_hi, core = fsdp // 4, lax.rem(fsdp // 2, 2), lax.rem(fsdp, 2)
    return {"x": x, "y": y_hi * 2 + y_lo, "z": z}, core


def device(at, core):
    y_hi, y_lo = at["y"] // 2, lax.rem(at["y"], 2)
    return (y_lo * 4 + at["z"], at["x"] * 4 + y_hi * 2 + core)


def moved(at, axis, by):
    return {**at, axis: lax.rem(at[axis] + by, 4)}


def whole():
    return pl.ds(0, 4)


def in_order(order):
    return AXES.index(order[1]) < AXES.index(order[2])


def spot(k, slot, a, b):
    return (slot, a, b) if in_order(REDUCE[k][2]) else (slot, b, a)


def kernel(
    hidden, weight, limit, cotangent,
    keys_out, grad_out, wgrad_out, ratio_out,
    w_in, codes, partial, hid, cot, keys_acc, keys_send, keys_recv, grad_stage, total,
    peak, peak_in,
    r1a, r1b, r1c, r2a, r2b, r2c, r3a, r3b, r3c,
    load_sem, swap_send, swap_recv, ag_send, ag_recv, rs_send, rs_recv, rep_send, rep_recv,
    peak_send, peak_recv, key_send, key_recv, grad_local, grad_send, grad_recv, out_sem,
):
    at, core = position()
    other = 1 - core
    partner = device(at, other)
    f32, bf16 = jnp.float32, jnp.bfloat16

    def remote(src, dst, send, recv, to):
        return pltpu.make_async_remote_copy(
            src_ref=src, dst_ref=dst, send_sem=send, recv_sem=recv, device_id=to, device_id_type=MESH
        )

    y_lo = lax.rem(at["y"], 2)
    piece_row = pl.multiple_of((y_lo * 4 + at["z"]) * ROWS, ROWS)
    load_w = pltpu.make_async_copy(weight.at[pl.ds(piece_row, ROWS)], w_in, load_sem.at[0])
    load_w.start()
    load_c = pltpu.make_async_copy(cotangent, cot.at[core], load_sem.at[1])
    load_c.start()

    def hid_cols(slot, which):
        return pl.ds(pl.multiple_of((slot * 2 + which) * BLOCK, BLOCK), BLOCK)

    load_h = []
    for s in range(SLOTS):
        load_h.append(
            pltpu.make_async_copy(hidden.at[:, hid_cols(s, core)], hid.at[s, core], load_sem.at[2 + s])
        )
        load_h[-1].start()

    barrier = pltpu.get_barrier_semaphore()
    pl.semaphore_signal(barrier, inc=1, device_id=partner, device_id_type=MESH)
    for axis in AXES:
        for j in (1, 2, 3):
            pl.semaphore_signal(barrier, inc=1, device_id=device(moved(at, axis, j), core), device_id_type=MESH)
    pl.semaphore_wait(barrier, 10)

    load_w.wait()
    lim = jnp.full((1, WIDTH), limit[0], f32)
    w = w_in[...].astype(f32)
    codes[at["x"], at["y"], at["z"]] = jnp.clip(w * (448.0 / lim), -448.0, 448.0).astype(bf16)

    def view(ref, where, cols):
        return ref.at[where["x"], where["y"], where["z"], slice(None), cols]

    def gather_direct(k, phase):
        start, size, order = GATHER[k]
        where = dict(at)
        for axis in order[:phase]:
            where[axis] = whole()
        src = view(codes, where, pl.ds(start, size))
        copies = []
        for j in (1, 2, 3):
            n = phase * 3 + j - 1
            copies.append(
                remote(src, src, ag_send.at[k, n], ag_recv.at[k, n], device(moved(at, order[phase], j), core))
            )
        return copies

    sent = []

    def start(copies):
        for copy in copies:
            copy.start()
            sent.append(copy)

    ag0 = [gather_direct(k, 0) for k in range(3)]
    for copies in ag0:
        start(copies)

    swaps = [remote(cotangent, cot.at[core], swap_send.at[0], swap_recv.at[0], partner)]
    for s in range(SLOTS):
        swaps.append(
            remote(hidden.at[:, hid_cols(s, other)], hid.at[s, core], swap_send.at[1 + s], swap_recv.at[1 + s], partner)
        )
    start(swaps)

    peak[0] = jnp.max(jnp.abs(w).reshape(ROWS // 8, 8, WIDTH // 128, 128).max(axis=0), axis=1)
    def peak_phase(p):
        targets = [partner] if p == 3 else [device(moved(at, AXES[p], j), core) for j in (1, 2, 3)]
        copies = [
            remote(peak.at[p], peak_in.at[p, j], peak_send.at[p, j], peak_recv.at[p, j], to)
            for j, to in enumerate(targets)
        ]
        start(copies)
        return copies

    def peak_join(p, copies):
        best = peak[p]
        for j, copy in enumerate(copies):
            copy.wait_recv()
            best = jnp.maximum(best, peak_in[p, j])
        peak[p + 1] = best

    peaks = peak_phase(0)

    for copies in ag0:
        for copy in copies:
            copy.wait_recv()
    ag1 = [gather_direct(k, 1) for k in range(3)]
    for copies in ag1:
        start(copies)
    peak_join(0, peaks)
    peaks = peak_phase(1)

    load_c.wait()
    swaps[0].wait_recv()

    @pl.loop(0, SLOTS)
    def _(s):
        pltpu.make_async_copy(hidden.at[:, hid_cols(0, core)], hid.at[s, core], load_sem.at[2 + s]).wait()
        remote(hidden.at[:, hid_cols(0, other)], hid.at[s, core], swap_send.at[1 + s], swap_recv.at[1 + s], partner).wait_recv()
        h = hid[s].reshape(2 * TOK, BLOCK)
        for n in range(0, WIDTH, 512):
            term = lax.dot_general(
                h, cot[:, :, pl.ds(n, 512)].reshape(2 * TOK, 512), (((0,), (0,)), ((), ())), preferred_element_type=f32
            )
            partial[s // 2, pl.ds(lax.rem(s, 2) * 2, 2), :, :, pl.ds(n, 512)] = term.astype(bf16).reshape(2, 4, ROWS, 512)

    first_in, second_in, third_in = (r1a, r1b, r1c), (r2a, r2b, r2c), (r3a, r3b, r3c)

    def chunk(k, by, half):
        first, size, order = REDUCE[k]
        where = {axis: whole() for axis in AXES}
        where[order[0]] = lax.rem(at[order[0]] + by, 4)
        if half is not None:
            where[order[1]] = pl.ds(2 * half, 2)
        return where, pl.ds(first, size)

    def ring(k, n, by, half, slot):
        first, size, order = REDUCE[k]
        where, cols = chunk(k, by, half)
        to = device(moved(at, order[0], 1 if n % 2 == 0 else 3), core)
        return remote(view(partial, where, cols), first_in[k].at[slot], rs_send.at[k, n], rs_recv.at[k, n], to)

    rs0 = []
    for k in range(3):
        rs0.append([ring(k, 0, 2, 0, 0), ring(k, 1, 2, 1, 1), ring(k, 2, 1, 1, 2), ring(k, 3, 3, 0, 3)])
    for n in range(4):
        start([rs0[k][n] for k in range(3)])

    def rows_loop(fn):
        @pl.loop(0, 8)
        def _(i):
            fn(i // 4, lax.rem(i, 4))

    def part(k, by, half, a, b):
        first, size, order = REDUCE[k]
        where = {order[0]: lax.rem(at[order[0]] + by, 4), order[1]: 2 * half + a, order[2]: b}
        return (where["x"], where["y"], where["z"], slice(None), pl.ds(first, size))

    def add_far(k, n, by, half):
        rs0[k][n].wait_recv()

        def one(a, b):
            at_piece = part(k, by, half, a, b)
            partial[at_piece] = (partial[at_piece].astype(f32) + first_in[k][spot(k, n, a, b)].astype(f32)).astype(bf16)

        rows_loop(one)

    def gather_ring(k, n, by, half):
        first, size, order = GATHER[k]
        where = {axis: whole() for axis in AXES}
        where[order[2]] = lax.rem(at[order[2]] + by, 4)
        where[order[0]] = pl.ds(2 * half, 2)
        src = view(codes, where, pl.ds(first, size))
        to = device(moved(at, order[2], 1 if n % 2 == 0 else 3), core)
        return remote(src, src, ag_send.at[k, 6 + n], ag_recv.at[k, 6 + n], to)

    for copies in ag1:
        for copy in copies:
            copy.wait_recv()
    ag2 = [
        [gather_ring(k, 0, 0, 0), gather_ring(k, 1, 0, 1), gather_ring(k, 2, 0, 1), gather_ring(k, 3, 0, 0),
         gather_ring(k, 4, 3, 0), gather_ring(k, 5, 1, 1)]
        for k in range(3)
    ]
    for n in range(4):
        start([ag2[k][n] for k in range(3)])

    peak_join(1, peaks)
    peaks = peak_phase(2)

    rs1 = []
    for k in range(3):
        rs1.append([ring(k, 4, 1, 0, 4), ring(k, 5, 3, 1, 5)])
        add_far(k, 0, 1, 0)
        start([rs1[k][0]])
        add_far(k, 1, 3, 1)
        start([rs1[k][1]])

    for k in range(3):
        ag2[k][0].wait_recv()
        start([ag2[k][4]])
        ag2[k][1].wait_recv()
        start([ag2[k][5]])

    peak_join(2, peaks)
    peaks = peak_phase(3)

    def reduce_direct(k, phase):
        first, size, order = REDUCE[k]
        landing = second_in if phase == 1 else third_in
        copies = []
        for j in (1, 2, 3):
            where = {order[0]: at[order[0]], order[1]: at[order[1]], order[2]: whole()}
            where[order[phase]] = lax.rem(at[order[phase]] + j, 4)
            n = 6 + (phase - 1) * 3 + j - 1
            copies.append(
                remote(view(partial, where, pl.ds(first, size)), landing[k].at[j - 1], rs_send.at[k, n],
                       rs_recv.at[k, n], device(moved(at, order[phase], j), core))
            )
        return copies

    rs2 = []
    for k in range(3):
        for copy in (rs0[k][2], rs0[k][3], rs1[k][0], rs1[k][1]):
            copy.wait_recv()
        for half in (0, 1):
            near, far = (3, 4) if half == 0 else (2, 5)

            def one(a, b, k=k, half=half, near=near, far=far):
                at_piece = part(k, 0, half, a, b)
                partial[at_piece] = (
                    partial[at_piece].astype(f32)
                    + first_in[k][spot(k, near, a, b)].astype(f32)
                    + first_in[k][spot(k, far, a, b)].astype(f32)
                ).astype(bf16)

            rows_loop(one)
        rs2.append(reduce_direct(k, 1))
        start(rs2[k])

    for k in range(3):
        for n in range(2, 6):
            ag2[k][n].wait_recv()

    unscale = limit[0] * (1.0 / 448.0)
    keys_acc[...] = jnp.zeros_like(keys_acc)

    def grad_cols(s):
        return pl.ds(pl.multiple_of((s * 2 + core) * BLOCK, BLOCK), BLOCK)

    def slots(lo, hi):
        @pl.loop(lo, hi)
        def _(s):
            w_s = codes[s // 2, pl.ds(lax.rem(s, 2) * 2, 2)].reshape(BLOCK, WIDTH)
            h = hid[s].reshape(2 * TOK, BLOCK)
            for n in range(0, WIDTH, 512):
                keys_acc[:, pl.ds(n, 512)] += jnp.dot(h, w_s[:, n : n + 512], preferred_element_type=f32)
            c_all = cot[...].reshape(2 * TOK, WIDTH)
            for n in range(0, BLOCK, 256):
                g = lax.dot_general(
                    c_all, w_s[n : n + 256], (((1,), (1,)), ((), ())), preferred_element_type=f32
                )
                grad_stage[s, :, :, pl.ds(n, 256)] = (g * unscale).astype(bf16).reshape(2, TOK, 256)
            pltpu.make_async_copy(grad_stage.at[s, core], grad_out.at[:, grad_cols(s)], grad_local.at[s]).start()
            remote(grad_stage.at[s, other], grad_out.at[:, grad_cols(s)], grad_send.at[s], grad_recv.at[s], partner).start()

    slots(0, 4)

    rs3 = []
    for k in range(3):
        first, size, order = REDUCE[k]
        for copy in rs2[k]:
            copy.wait_recv()

        @pl.loop(0, 4)
        def _(b, k=k, first=first, size=size, order=order):
            where = {order[0]: at[order[0]], order[1]: at[order[1]], order[2]: b}
            at_piece = (where["x"], where["y"], where["z"], slice(None), pl.ds(first, size))
            acc = partial[at_piece].astype(f32)
            for j in range(3):
                acc += second_in[k][j, b].astype(f32)
            partial[at_piece] = acc.astype(bf16)

        rs3.append(reduce_direct(k, 2))
        start(rs3[k])

    slots(4, 8)

    keys_send[...] = keys_acc[pl.ds(pl.multiple_of(other * TOK, TOK), TOK)].astype(bf16)
    key_copy = remote(keys_send, keys_recv, key_send.at[0], key_recv.at[0], partner)
    start([key_copy])

    for k in range(3):
        first, size, order = REDUCE[k]
        for copy in rs3[k]:
            copy.wait_recv()
        acc = partial[at["x"], at["y"], at["z"], :, pl.ds(first, size)].astype(f32)
        for j in range(3):
            acc += third_in[k][j].astype(f32)
        total[:, pl.ds(first, size)] = (acc * (32768.0**-0.5)).astype(bf16)

    def piece(lo, z):
        return wgrad_out.at[pl.ds(pl.multiple_of((lo * 4 + z) * ROWS, ROWS), ROWS)]

    beside = {**at, "y": at["y"] + 1 - 2 * y_lo}
    own = pltpu.make_async_copy(total, piece(y_lo, at["z"]), out_sem.at[0])
    own.start()
    rep0 = [
        remote(total, piece(y_lo, at["z"]), rep_send.at[0], rep_recv.at[0], device(beside, core)),
        remote(total, piece(y_lo, at["z"]), rep_send.at[1], rep_recv.at[1], device(moved(at, "z", 1), core)),
        remote(total, piece(y_lo, at["z"]), rep_send.at[2], rep_recv.at[2], device(moved(at, "z", 3), core)),
        remote(total, piece(y_lo, at["z"]), rep_send.at[3], rep_recv.at[3], device(moved(at, "z", 2), core)),
    ]
    start(rep0)

    peak_join(3, peaks)
    ratio_out[0] = jnp.max(peak[4] / jnp.full((8, 128), limit[0], f32))
    key_copy.wait_recv()
    mine = keys_acc[pl.ds(pl.multiple_of(core * TOK, TOK), TOK)] + keys_recv[...].astype(f32)
    keys_send_2 = (mine * unscale).astype(bf16)
    key_copy.wait_send()
    keys_send[...] = keys_send_2
    sent[:] = [copy for copy in sent if copy is not key_copy]
    out_keys = pltpu.make_async_copy(keys_send, keys_out, out_sem.at[1])
    out_keys.start()

    z_far = lax.rem(at["z"] + 2, 4)
    rep0[0].wait_recv()
    across = piece(1 - y_lo, at["z"])
    rep1 = [
        remote(across, across, rep_send.at[4], rep_recv.at[4], device(moved(at, "z", 1), core)),
        remote(across, across, rep_send.at[5], rep_recv.at[5], device(moved(at, "z", 3), core)),
    ]
    start(rep1)
    rep0[3].wait_recv()
    far = piece(y_lo, z_far)
    rep1.append(remote(far, far, rep_send.at[6], rep_recv.at[6], device(beside, core)))
    start(rep1[2:])
    for copy in (rep0[1], rep0[2], *rep1):
        copy.wait_recv()

    for s in range(SLOTS):
        pltpu.make_async_copy(grad_stage.at[s, core], grad_out.at[:, grad_cols(s)], grad_local.at[s]).wait()
        remote(grad_stage.at[s, other], grad_out.at[:, grad_cols(s)], grad_send.at[s], grad_recv.at[s], partner).wait()
    own.wait()
    out_keys.wait()
    for copy in sent:
        copy.wait_send()


def landing(k, phase):
    first, size, order = REDUCE[k]
    if phase == 0:
        return pltpu.VMEM((*spot(k, 6, 2, 4), ROWS, size), jnp.bfloat16)
    if phase == 1:
        return pltpu.VMEM((3, 4, ROWS, size), jnp.bfloat16)
    return pltpu.VMEM((3, ROWS, size), jnp.bfloat16)


def body(hidden_states, key_weight, previous_peak, key_cotangent):
    bf16, f32 = jnp.bfloat16, jnp.float32
    any_space = pl.BlockSpec(memory_space=pl.ANY)
    smem = pl.BlockSpec(memory_space=pltpu.SMEM)
    dma = pltpu.SemaphoreType.DMA
    return pl.pallas_call(
        kernel,
        out_shape=(
            jax.ShapeDtypeStruct((TOK, WIDTH), bf16),
            jax.ShapeDtypeStruct((TOK, 2 * SLOTS * BLOCK), bf16),
            jax.ShapeDtypeStruct((BLOCK, WIDTH), bf16),
            jax.ShapeDtypeStruct((1,), f32),
        ),
        in_specs=[any_space, any_space, smem, any_space],
        out_specs=(any_space, any_space, any_space, smem),
        scratch_shapes=[
            pltpu.VMEM((ROWS, WIDTH), bf16),
            pltpu.VMEM((4, 4, 4, ROWS, WIDTH), bf16),
            pltpu.VMEM((4, 4, 4, ROWS, WIDTH), bf16),
            pltpu.VMEM((SLOTS, 2, TOK, BLOCK), bf16),
            pltpu.VMEM((2, TOK, WIDTH), bf16),
            pltpu.VMEM((2 * TOK, WIDTH), f32),
            pltpu.VMEM((TOK, WIDTH), bf16),
            pltpu.VMEM((TOK, WIDTH), bf16),
            pltpu.VMEM((SLOTS, 2, TOK, BLOCK), bf16),
            pltpu.VMEM((ROWS, WIDTH), bf16),
            pltpu.VMEM((5, 8, 128), f32),
            pltpu.VMEM((4, 3, 8, 128), f32),
            *[landing(k, phase) for phase in range(3) for k in range(3)],
            dma((2 + SLOTS,)),
            dma((1 + SLOTS,)),
            dma((1 + SLOTS,)),
            dma((3, 12)),
            dma((3, 12)),
            dma((3, 12)),
            dma((3, 12)),
            dma((7,)),
            dma((7,)),
            dma((4, 3)),
            dma((4, 3)),
            dma((1,)),
            dma((1,)),
            dma((SLOTS,)),
            dma((SLOTS,)),
            dma((SLOTS,)),
            dma((2,)),
        ],
        compiler_params=pltpu.CompilerParams(
            collective_id=0, has_side_effects=True, vmem_limit_bytes=58 * 2**20
        ),
    )(hidden_states, key_weight, previous_peak, key_cotangent)


def solution(mesh):
    in_specs = (P(("replica", "fsdp"), None), P("fsdp", None), P(), P(("replica", "fsdp"), None))
    out_specs = (P(("replica", "fsdp"), None), P(("replica", "fsdp"), None), P("fsdp", None), P())
    return jax.shard_map(body, mesh=mesh, in_specs=in_specs, out_specs=out_specs, check_vma=False)
```

time: 400 us -> 109 us (0.27)
  waiting for transfers between devices: 301 us -> 0 us
  Pallas kernels: 0 us -> 98.5 us
  matrix products: 34.3 us -> 0 us
  blocking collectives: 34 us -> 0 us
  between operations: 16.2 us -> 3.04 us
  other arithmetic: 4.27 us -> 0 us
    reduce_scatter x1 -> x0, waiting for transfers between devices: 150 us -> none  [body(): lax.psum_scatter(lax.dot_general(hidden_states, key_cotangent, (((0,), (0...]
    all_gather x1 -> x0, waiting for transfers between devices: 111 us -> none  [body(): gathered = lax.all_gather(source, 'fsdp', axis=0, tiled=True)]
    pallas_call x0 -> x1, Pallas kernels: none -> 98.5 us  [body(): pl.pallas_call(kernel, out_shape=(jax.ShapeDtypeStruct((TOK, WIDTH), bf16...]
    psum x1 -> x0, waiting for transfers between devices: 40.6 us -> none  [body(): total = lax.psum(group, 'replica').astype(jnp.float32)]
    dot_general x3 -> x0, matrix products: 34.3 us -> none  [the longest x1 12.3 us: body(): lax.dot_general(key_cotangent, gathered, (((1,), (1,)), ((), ())), prefer...]
    pmax x1 -> x0, blocking collectives: 34 us -> none  [body(): peak = lax.pmax(local_peak, 'fsdp')]
    unnamed x6 -> x5, local copies, waits for them, and re-layouts: 8.31 us -> 7.57 us
  transfers between devices with their start and end apart: 3 -> 0, of which waited for: 3 -> 0; matrix products, arithmetic and copies ran while one was open for 1% -> 0% of each run, Pallas kernels for 0% -> 0%
where the time goes in v1:
time: 109 us
  Pallas kernels  98.5 us (90%)
  local copies, waits for them, and re-layouts  7.57 us (7%)
  between operations  3.04 us (3%)
    pallas_call x1, Pallas kernels, body(): pl.pallas_call(kernel, out_shape=(jax.ShapeDtypeStruct((TOK, WIDTH), bf16...  98.5 us
    unnamed x5, local copies, waits for them, and re-layouts  7.57 us

profile of v1, /device:TPU:0, one launch (start us, length us, event | category | flops | bytes accessed | tf_op | source)
XLA Modules:
  0.0 109.1 jit_solution(9704839376386538885)
XLA Ops:
  1.3 98.5 %shard_map.75 = (bf16[256,1024]{1,0:T(8,128)(2,1)}, bf16[256,8192]{1,0:T(8,128)(2,1)}, bf16[512,1024]{1,0:T(8,128)(2,1)}, f32[1]{0:T(128)}) custom-call(bf16[256,8192]{1,0:T(8,128)(2,1)} %hidden.1, bf16[512,1024]{1,0:T(8,128)(2,1)} %weight.1, f32[1]{0:T(128)S(6)} %copy.12.limit, bf16[256,1024]{1,0:T(8,128)(2,1)} %cotangent.1), custom_call_target="tpu_custom_call" | custom-call | tf_op jit(solution)/shard_map/pallas_call | solution.py:412
  99.8 1.9 %copy.13 = bf16[256,1024]{1,0:T(8,128)(2,1)} copy(bf16[256,1024]{1,0:T(8,128)(2,1)} %get-tuple-element.8) | data formatting | bytes 1048576
  101.6 0.0 copy-start
  101.6 4.7 %copy.14 = bf16[256,8192]{1,0:T(8,128)(2,1)} copy(bf16[256,8192]{1,0:T(8,128)(2,1)} %get-tuple-element.9) | data formatting | bytes 8388608
  106.4 0.0 copy-done
  106.4 1.0 copy.15
Async XLA Ops:
  101.6 4.7 %copy-start = (bf16[512,1024]{1,0:T(8,128)(2,1)S(1)}, bf16[512,1024]{1,0:T(8,128)(2,1)}, u32[]{:S(2)}) copy-start(bf16[512,1024]{1,0:T(8,128)(2,1)} %get-tuple-element.10) | copy-start | bytes 3145732

commit v2 on v0

v2 whole, which is shorter than its diff:
```python
import jax
import jax.numpy as jnp
from jax import lax
from jax.experimental import pallas as pl
from jax.experimental.pallas import tpu as pltpu
from jax.sharding import PartitionSpec as P

MESH = pl.DeviceIdType.MESH
AXES = ("x", "y", "z")
ROWS = 64
WIDTH = 1024
TOK = 256
SLOTS = 8
BLOCK = 512
GATHER = ((0, 256, ("z", "y", "x")), (256, 384, ("z", "x", "y")), (640, 384, ("y", "x", "z")))
REDUCE = (
    (0, 640, 384, ("z", "x", "y")),
    (0, 0, 384, ("x", "y", "z")),
    (0, 384, 256, ("y", "z", "x")),
    (1, 640, 384, ("z", "y", "x")),
    (1, 0, 256, ("x", "z", "y")),
    (1, 256, 384, ("y", "x", "z")),
)
GROUPS = len(REDUCE)
HALF = ROWS // 2


def position():
    replica, fsdp = lax.axis_index("replica"), lax.axis_index("fsdp")
    y_lo, z = replica // 4, lax.rem(replica, 4)
    x, y_hi, core = fsdp // 4, lax.rem(fsdp // 2, 2), lax.rem(fsdp, 2)
    return {"x": x, "y": y_hi * 2 + y_lo, "z": z}, core


def device(at, core):
    y_hi, y_lo = at["y"] // 2, lax.rem(at["y"], 2)
    return (y_lo * 4 + at["z"], at["x"] * 4 + y_hi * 2 + core)


def moved(at, axis, by):
    return {**at, axis: lax.rem(at[axis] + by, 4)}


def whole():
    return pl.ds(0, 4)


def spot(k, slot, a, b):
    order = REDUCE[k][3]
    return (slot, a, b) if AXES.index(order[1]) < AXES.index(order[2]) else (slot, b, a)


def half_rows(half):
    return pl.ds(half * HALF, HALF)


def kernel(hidden, weight, limit, cotangent, keys_out, grad_out, wgrad_out, ratio_out, *scratch):
    (w_in, codes, partial, hid, cot, keys_acc, keys_send, keys_recv, grad_stage, peak, peak_in) = scratch[:11]
    landings = scratch[11 : 11 + 3 * GROUPS]
    first_in, second_in, third_in = (landings[n * GROUPS : (n + 1) * GROUPS] for n in range(3))
    (load_sem, swap_send, swap_recv, ag_send, ag_recv, rs_send, rs_recv, rep_send, rep_recv,
     peak_send, peak_recv, key_send, key_recv, grad_send, grad_recv) = scratch[11 + 3 * GROUPS :]

    at, core = position()
    other = 1 - core
    partner = device(at, other)
    f32, bf16 = jnp.float32, jnp.bfloat16
    y_lo = lax.rem(at["y"], 2)

    def remote(src, dst, send, recv, to):
        return pltpu.make_async_remote_copy(
            src_ref=src, dst_ref=dst, send_sem=send, recv_sem=recv, device_id=to, device_id_type=MESH
        )

    sent = []

    def start(copies):
        for copy in copies:
            copy.start()
            sent.append(copy)

    def hid_cols(slot, which):
        return pl.ds(pl.multiple_of((slot * 2 + which) * BLOCK, BLOCK), BLOCK)

    load_w = pltpu.make_async_copy(
        weight.at[pl.ds(pl.multiple_of(y_lo * 4 * ROWS, 4 * ROWS), 4 * ROWS)], w_in, load_sem.at[0]
    )
    load_w.start()
    load_c = pltpu.make_async_copy(cotangent, cot.at[0], load_sem.at[1])
    load_c.start()
    for s in range(SLOTS):
        pltpu.make_async_copy(hidden.at[:, hid_cols(s, core)], hid.at[s, 0], load_sem.at[2 + s]).start()

    barrier = pltpu.get_barrier_semaphore()
    pl.semaphore_signal(barrier, inc=1, device_id=partner, device_id_type=MESH)
    for axis in AXES:
        for j in (1, 2, 3):
            pl.semaphore_signal(barrier, inc=1, device_id=device(moved(at, axis, j), core), device_id_type=MESH)

    load_w.wait()
    lim = jnp.full((1, WIDTH), limit[0], f32)
    scale = 448.0 / lim

    def quantize(w, cols):
        return jnp.clip(w.astype(f32) * scale[:, cols], -448.0, 448.0).astype(bf16)

    split = GATHER[2][0]
    for z in range(4):
        codes[at["x"], at["y"], z, :, :split] = quantize(w_in[z * ROWS : (z + 1) * ROWS, :split], slice(0, split))
    own_rows = w_in[pl.ds(pl.multiple_of(at["z"] * ROWS, ROWS), ROWS), :]
    codes[at["x"], at["y"], at["z"], :, split:] = quantize(own_rows[:, split:], slice(split, WIDTH))

    pl.semaphore_wait(barrier, 10)

    def view(ref, where, rows, cols):
        return ref.at[where["x"], where["y"], where["z"], rows, cols]

    def gather_direct(k, phase):
        first, size, order = GATHER[k]
        where = dict(at)
        for axis in order[:phase]:
            where[axis] = whole()
        src = view(codes, where, slice(None), pl.ds(first, size))
        return [
            remote(src, src, ag_send.at[k, phase * 3 + j - 1], ag_recv.at[k, phase * 3 + j - 1],
                   device(moved(at, order[phase], j), core))
            for j in (1, 2, 3)
        ]

    ag_first = gather_direct(2, 0)
    start(ag_first)
    ag_mid = [gather_direct(0, 1), gather_direct(1, 1), gather_direct(2, 1)]
    start(ag_mid[0] + ag_mid[1])

    swaps = [remote(cotangent, cot.at[1], swap_send.at[0], swap_recv.at[0], partner)]
    for s in range(SLOTS):
        swaps.append(
            remote(hidden.at[:, hid_cols(s, other)], hid.at[s, 1], swap_send.at[1 + s], swap_recv.at[1 + s], partner)
        )
    start(swaps)

    peak[0] = jnp.max(
        jnp.abs(own_rows.astype(f32)).reshape(ROWS // 8, 8, WIDTH // 128, 128).max(axis=0), axis=1
    )

    def peak_phase(p):
        targets = [partner] if p == 3 else [device(moved(at, AXES[p], j), core) for j in (1, 2, 3)]
        copies = [
            remote(peak.at[p], peak_in.at[p, j], peak_send.at[p, j], peak_recv.at[p, j], to)
            for j, to in enumerate(targets)
        ]
        start(copies)
        return copies

    def peak_join(p, copies):
        best = peak[p]
        for j, copy in enumerate(copies):
            copy.wait_recv()
            best = jnp.maximum(best, peak_in[p, j])
        peak[p + 1] = best

    peaks = peak_phase(0)

    for copy in ag_first:
        copy.wait_recv()
    start(ag_mid[2])

    def partials(first, size, arrive):
        @pl.loop(0, SLOTS)
        def _(s):
            if arrive:
                pltpu.make_async_copy(hidden.at[:, hid_cols(0, core)], hid.at[s, 0], load_sem.at[2 + s]).wait()
                remote(
                    hidden.at[:, hid_cols(0, other)], hid.at[s, 1], swap_send.at[1 + s], swap_recv.at[1 + s], partner
                ).wait_recv()
            term = lax.dot_general(
                hid[s].reshape(2 * TOK, BLOCK), cot[:, :, first : first + size].reshape(2 * TOK, size),
                (((0,), (0,)), ((), ())), preferred_element_type=f32,
            )
            partial[s // 2, pl.ds(lax.rem(s, 2) * 2, 2), :, :, first : first + size] = term.astype(bf16).reshape(
                2, 4, ROWS, size
            )

    def ring(k, n, by, half, slot):
        rows, first, size, order = REDUCE[k]
        where = {order[0]: lax.rem(at[order[0]] + by, 4), order[1]: pl.ds(2 * half, 2), order[2]: whole()}
        to = device(moved(at, order[0], 1 if n % 2 == 0 else 3), core)
        return remote(
            view(partial, where, half_rows(rows), pl.ds(first, size)), first_in[k].at[slot],
            rs_send.at[k, n], rs_recv.at[k, n], to,
        )

    rs_ring = [
        [ring(k, 0, 2, 0, 0), ring(k, 1, 2, 1, 1), ring(k, 2, 1, 1, 2), ring(k, 3, 3, 0, 3),
         ring(k, 4, 1, 0, 4), ring(k, 5, 3, 1, 5)]
        for k in range(GROUPS)
    ]

    def ring_begin(groups):
        for k in groups:
            start(rs_ring[k][0:2])
        for k in groups:
            start(rs_ring[k][2:4])

    def part(k, by, half, a, b):
        rows, first, size, order = REDUCE[k]
        where = {order[0]: lax.rem(at[order[0]] + by, 4), order[1]: 2 * half + a, order[2]: b}
        return (where["x"], where["y"], where["z"], half_rows(rows), pl.ds(first, size))

    def add_landed(k, by, half, slots):
        @pl.loop(0, 4)
        def _(b):
            for a in (0, 1):
                index = part(k, by, half, a, b)
                acc = partial[index].astype(f32)
                for slot in slots:
                    acc += first_in[k][spot(k, slot, a, b)].astype(f32)
                partial[index] = acc.astype(bf16)

    def ring_forward(k):
        for n, by, half in ((0, 1, 0), (1, 3, 1)):
            rs_ring[k][n].wait_recv()
            add_landed(k, by, half, (n,))
            start([rs_ring[k][4 + n]])

    def reduce_direct(k, phase):
        rows, first, size, order = REDUCE[k]
        landing = second_in if phase == 1 else third_in
        copies = []
        for j in (1, 2, 3):
            where = {order[0]: at[order[0]], order[1]: at[order[1]], order[2]: whole()}
            where[order[phase]] = lax.rem(at[order[phase]] + j, 4)
            n = 6 + (phase - 1) * 3 + j - 1
            copies.append(
                remote(view(partial, where, half_rows(rows), pl.ds(first, size)), landing[k].at[j - 1],
                       rs_send.at[k, n], rs_recv.at[k, n], device(moved(at, order[phase], j), core))
            )
        return copies

    rs_second = [reduce_direct(k, 1) for k in range(GROUPS)]
    rs_third = [reduce_direct(k, 2) for k in range(GROUPS)]

    def ring_end(k):
        for n in range(2, 6):
            rs_ring[k][n].wait_recv()
        add_landed(k, 0, 0, (3, 4))
        add_landed(k, 0, 1, (2, 5))
        start(rs_second[k])

    def second_end(k):
        rows, first, size, order = REDUCE[k]
        for copy in rs_second[k]:
            copy.wait_recv()

        @pl.loop(0, 4)
        def _(b):
            where = {order[0]: at[order[0]], order[1]: at[order[1]], order[2]: b}
            index = (where["x"], where["y"], where["z"], half_rows(rows), pl.ds(first, size))
            acc = partial[index].astype(f32)
            for j in range(3):
                acc += second_in[k][j, b].astype(f32)
            partial[index] = acc.astype(bf16)

        start(rs_third[k])

    def piece(half, lo, z):
        return pl.ds(pl.multiple_of((lo * 4 + z) * ROWS + half * HALF, HALF), HALF)

    def third_end(k):
        rows, first, size, order = REDUCE[k]
        for copy in rs_third[k]:
            copy.wait_recv()
        acc = partial[at["x"], at["y"], at["z"], half_rows(rows), pl.ds(first, size)].astype(f32)
        for j in range(3):
            acc += third_in[k][j].astype(f32)
        wgrad_out[piece(rows, y_lo, at["z"]), pl.ds(first, size)] = (acc * (32768.0**-0.5)).astype(bf16)

    beside = device({**at, "y": at["y"] + 1 - 2 * y_lo}, core)

    def spread(half, n, rows, to):
        src = wgrad_out.at[rows]
        return remote(src, src, rep_send.at[half, n], rep_recv.at[half, n], to)

    near = [device(moved(at, "z", j), core) for j in (1, 3, 2)]
    rep = []
    for half in (0, 1):
        mine, across = piece(half, y_lo, at["z"]), piece(half, 1 - y_lo, at["z"])
        far = piece(half, y_lo, lax.rem(at["z"] + 2, 4))
        rep.append(
            [spread(half, 0, mine, beside)]
            + [spread(half, 1 + n, mine, to) for n, to in enumerate(near)]
            + [spread(half, 4, across, near[0]), spread(half, 5, across, near[1]), spread(half, 6, far, beside)]
        )

    def spread_more(half):
        rep[half][0].wait_recv()
        start(rep[half][4:6])
        rep[half][3].wait_recv()
        start(rep[half][6:7])

    def gather_ring(k, n, by, half):
        first, size, order = GATHER[k]
        where = {axis: whole() for axis in AXES}
        where[order[2]] = lax.rem(at[order[2]] + by, 4)
        where[order[0]] = pl.ds(2 * half, 2)
        src = view(codes, where, slice(None), pl.ds(first, size))
        to = device(moved(at, order[2], 1 if n % 2 == 0 else 3), core)
        return remote(src, src, ag_send.at[k, 6 + n], ag_recv.at[k, 6 + n], to)

    ag_ring = [
        [gather_ring(k, 0, 0, 0), gather_ring(k, 1, 0, 1), gather_ring(k, 2, 0, 1), gather_ring(k, 3, 0, 0),
         gather_ring(k, 4, 3, 0), gather_ring(k, 5, 1, 1)]
        for k in range(3)
    ]

    def gather_last(k):
        for copy in ag_mid[k]:
            copy.wait_recv()
        start(ag_ring[k][:4])

    def gather_forward(k):
        for n in (0, 1):
            ag_ring[k][n].wait_recv()
            start([ag_ring[k][4 + n]])

    unscale = limit[0] * (1.0 / 448.0)

    def matmuls(lo, hi):
        @pl.loop(lo, hi)
        def _(s):
            w_s = codes[s // 2, pl.ds(lax.rem(s, 2) * 2, 2)].reshape(BLOCK, WIDTH)
            h = hid[s].reshape(2 * TOK, BLOCK)
            for n in range(0, WIDTH, 512):
                keys_acc[:, n : n + 512] += jnp.dot(h, w_s[:, n : n + 512], preferred_element_type=f32)
            c_all = cot[...].reshape(2 * TOK, WIDTH)
            for n in range(0, BLOCK, 256):
                g = lax.dot_general(c_all, w_s[n : n + 256], (((1,), (1,)), ((), ())), preferred_element_type=f32)
                g = (g * unscale).astype(bf16)
                grad_stage[s, :, n : n + 256] = g[TOK:]
                grad_out[:, pl.ds(pl.multiple_of((s * 2 + core) * BLOCK + n, 256), 256)] = g[:TOK]
            remote(
                grad_stage.at[s], grad_out.at[:, hid_cols(s, core)], grad_send.at[s], grad_recv.at[s], partner
            ).start()

    load_c.wait()
    swaps[0].wait_recv()
    partials(512, 512, True)
    ring_begin((0, 3))
    partials(0, 512, False)
    ring_begin((1, 2))
    ring_begin((4, 5))
    peak_join(0, peaks)
    peaks = peak_phase(1)
    for k in range(3):
        gather_last(k)
    keys_acc[...] = jnp.zeros_like(keys_acc)
    for k in range(GROUPS):
        ring_forward(k)
    peak_join(1, peaks)
    peaks = peak_phase(2)
    for k in range(3):
        gather_forward(k)
    for k in range(GROUPS):
        ring_end(k)
    peak_join(2, peaks)
    peaks = peak_phase(3)
    for k in range(3):
        for copy in ag_ring[k][2:]:
            copy.wait_recv()
    matmuls(0, 2)
    for k in (0, 1, 2):
        second_end(k)
    matmuls(2, 4)
    for k in (3, 4, 5):
        second_end(k)
    matmuls(4, 6)
    for k in (0, 1, 2):
        third_end(k)
    start(rep[0][:4])
    matmuls(6, 8)
    for k in (3, 4, 5):
        third_end(k)
    start(rep[1][:4])
    keys_send[...] = keys_acc[TOK:].astype(bf16)
    key_copy = remote(keys_send, keys_recv, key_send.at[0], key_recv.at[0], partner)
    start([key_copy])
    spread_more(0)
    peak_join(3, peaks)
    ratio_out[0] = jnp.max(peak[4] / jnp.full((8, 128), limit[0], f32))
    key_copy.wait_recv()
    keys_out[...] = ((keys_acc[:TOK] + keys_recv[...].astype(f32)) * unscale).astype(bf16)
    spread_more(1)

    for s in range(SLOTS):
        remote(grad_stage.at[s], grad_out.at[:, hid_cols(s, core)], grad_send.at[s], grad_recv.at[s], partner).wait()
    for half in (0, 1):
        for n in (1, 2, 4, 5, 6):
            rep[half][n].wait_recv()
    for copy in sent:
        copy.wait_send()


def place(keys, grad, wgrad, keys_out, grad_out, wgrad_out, sem):
    copies = [
        pltpu.make_async_copy(src, dst, sem.at[n])
        for n, (src, dst) in enumerate(((grad, grad_out), (wgrad, wgrad_out), (keys, keys_out)))
    ]
    for copy in copies:
        copy.start()
    for copy in copies:
        copy.wait()


def landing(k, phase):
    size = REDUCE[k][2]
    shape = (spot(k, 6, 2, 4), (3, 4), (3,))[phase]
    return pltpu.VMEM((*shape, HALF, size), jnp.bfloat16)


def body(hidden_states, key_weight, previous_peak, key_cotangent):
    bf16, f32 = jnp.bfloat16, jnp.float32
    any_space = pl.BlockSpec(memory_space=pl.ANY)
    hbm = pl.BlockSpec(memory_space=pltpu.HBM)
    vmem = pl.BlockSpec(memory_space=pltpu.VMEM)
    smem = pl.BlockSpec(memory_space=pltpu.SMEM)
    dma = pltpu.SemaphoreType.DMA
    shapes = ((TOK, WIDTH), (TOK, 2 * SLOTS * BLOCK), (BLOCK, WIDTH))
    *results, ratio = pl.pallas_call(
        kernel,
        out_shape=(*[pltpu.VMEM(shape, bf16) for shape in shapes], jax.ShapeDtypeStruct((1,), f32)),
        in_specs=[hbm, hbm, smem, hbm],
        out_specs=(vmem, vmem, vmem, smem),
        scratch_shapes=[
            pltpu.VMEM((4 * ROWS, WIDTH), bf16),
            pltpu.VMEM((4, 4, 4, ROWS, WIDTH), bf16),
            pltpu.VMEM((4, 4, 4, ROWS, WIDTH), bf16),
            pltpu.VMEM((SLOTS, 2, TOK, BLOCK), bf16),
            pltpu.VMEM((2, TOK, WIDTH), bf16),
            pltpu.VMEM((2 * TOK, WIDTH), f32),
            pltpu.VMEM((TOK, WIDTH), bf16),
            pltpu.VMEM((TOK, WIDTH), bf16),
            pltpu.VMEM((SLOTS, TOK, BLOCK), bf16),
            pltpu.VMEM((5, 8, 128), f32),
            pltpu.VMEM((4, 3, 8, 128), f32),
            *[landing(k, phase) for phase in range(3) for k in range(GROUPS)],
            dma((2 + SLOTS,)),
            dma((1 + SLOTS,)),
            dma((1 + SLOTS,)),
            dma((3, 12)),
            dma((3, 12)),
            dma((GROUPS, 12)),
            dma((GROUPS, 12)),
            dma((2, 7)),
            dma((2, 7)),
            dma((4, 3)),
            dma((4, 3)),
            dma((1,)),
            dma((1,)),
            dma((SLOTS,)),
            dma((SLOTS,)),
        ],
        compiler_params=pltpu.CompilerParams(
            collective_id=0, has_side_effects=True, vmem_limit_bytes=44 * 2**20
        ),
    )(
        pltpu.with_memory_space_constraint(hidden_states, pltpu.HBM),
        pltpu.with_memory_space_constraint(key_weight, pltpu.HBM),
        previous_peak,
        pltpu.with_memory_space_constraint(key_cotangent, pltpu.HBM),
    )
    keys, grad, wgrad = pl.pallas_call(
        place,
        out_shape=tuple(jax.ShapeDtypeStruct(shape, bf16) for shape in shapes),
        in_specs=[any_space] * 3,
        out_specs=(any_space,) * 3,
        scratch_shapes=[dma((3,))],
        compiler_params=pltpu.CompilerParams(vmem_limit_bytes=2**20),
    )(*[pltpu.with_memory_space_constraint(array, pltpu.VMEM) for array in results])
    return keys, grad, wgrad, ratio


def solution(mesh):
    in_specs = (P(("replica", "fsdp"), None), P("fsdp", None), P(), P(("replica", "fsdp"), None))
    out_specs = (P(("replica", "fsdp"), None), P(("replica", "fsdp"), None), P("fsdp", None), P())
    return jax.shard_map(body, mesh=mesh, in_specs=in_specs, out_specs=out_specs, check_vma=False)
```

time: 400 us -> 99.3 us (0.25)
  waiting for transfers between devices: 301 us -> 0 us
  Pallas kernels: 0 us -> 95.3 us
  matrix products: 34.3 us -> 0 us
  blocking collectives: 34 us -> 0 us
  between operations: 16.2 us -> 3.05 us
  local copies, waits for them, and re-layouts: 8.31 us -> 0 us
  other arithmetic: 4.27 us -> 0 us
    reduce_scatter x1 -> x0, waiting for transfers between devices: 150 us -> none  [body(): lax.psum_scatter(lax.dot_general(hidden_states, key_cotangent, (((0,), (0...]
    all_gather x1 -> x0, waiting for transfers between devices: 111 us -> none  [body(): gathered = lax.all_gather(source, 'fsdp', axis=0, tiled=True)]
    pallas_call x0 -> x2, Pallas kernels: none -> 95.3 us  [the longest x1 92.8 us: body(): pl.pallas_call(kernel, out_shape=(*[pltpu.VMEM(shape, bf16) for shape in...]
    psum x1 -> x0, waiting for transfers between devices: 40.6 us -> none  [body(): total = lax.psum(group, 'replica').astype(jnp.float32)]
    dot_general x3 -> x0, matrix products: 34.3 us -> none  [the longest x1 12.3 us: body(): lax.dot_general(key_cotangent, gathered, (((1,), (1,)), ((), ())), prefer...]
    pmax x1 -> x0, blocking collectives: 34 us -> none  [body(): peak = lax.pmax(local_peak, 'fsdp')]
    unnamed x6 -> x0, local copies, waits for them, and re-layouts: 8.31 us -> none
  transfers between devices with their start and end apart: 3 -> 0, of which waited for: 3 -> 0; matrix products, arithmetic and copies ran while one was open for 1% -> 0% of each run, Pallas kernels for 0% -> 0%
where the time goes in v2:
time: 99.3 us; the launch traced here: 98.3 us
  Pallas kernels  95.3 us (96%)
  between operations  3.05 us (3%)
    pallas_call x1, Pallas kernels, body(): pl.pallas_call(kernel, out_shape=(*[pltpu.VMEM(shape, bf16) for shape in...  92.8 us
    pallas_call x1, Pallas kernels, body(): pl.pallas_call(place, out_shape=tuple((jax.ShapeDtypeStruct(shape, bf16)...  2.52 us

profile of v2, /device:TPU:0, one launch (start us, length us, event | category | flops | bytes accessed | tf_op | source)
XLA Modules:
  0.0 98.3 jit_solution(14160456233657892540)
XLA Ops:
  1.3 92.8 %shard_map.75 = (bf16[256,1024]{1,0:T(8,128)(2,1)S(1)}, bf16[256,8192]{1,0:T(8,128)(2,1)S(1)}, bf16[512,1024]{1,0:T(8,128)(2,1)S(1)}, f32[1]{0:T(128)}) custom-call(bf16[256,8192]{1,0:T(8,128)(2,1)} %hidden.1, bf16[512,1024]{1,0:T(8,128)(2,1)} %weight.1, f32[1]{0:T(128)S(6)} %copy.9.limit, bf16[256,1024]{1,0:T(8,128)(2,1)} %cotangent.1), custom_call_target="tpu_custom_call" | custom-call | tf_op jit(solution)/shard_map/pallas_call | solution.py:428
  94.0 2.5 %shard_map.76 = (bf16[256,1024]{1,0:T(8,128)(2,1)}, bf16[256,8192]{1,0:T(8,128)(2,1)}, bf16[512,1024]{1,0:T(8,128)(2,1)}) custom-call(bf16[256,1024]{1,0:T(8,128)(2,1)S(1)} %get-tuple-element.11.keys, bf16[256,8192]{1,0:T(8,128)(2,1)S(1)} %get-tuple-element.12.grad, bf16[512,1024]{1,0:T(8,128)(2,1)S(1)} %get-tuple-element.13.wgrad), custom_call_target="tpu_custom_call" | custom-call | tf_op jit(solution)/shard_map/pallas_call | solution.py:471

commit v3 on v2

--- a/solution.py
+++ b/solution.py
@@ -12,14 +12,32 @@
 TOK = 256
 SLOTS = 8
 BLOCK = 512
-GATHER = ((0, 256, ("z", "y", "x")), (256, 384, ("z", "x", "y")), (640, 384, ("y", "x", "z")))
+GATHER = (
+    (0, 384, ("z", "y", "x")),
+    (384, 256, ("x", "z", "y")),
+    (640, 384, ("y", "x", "z")),
+)
 REDUCE = (
-    (0, 640, 384, ("z", "x", "y")),
+    (0, 640, 384, ("z", "y", "x")),
     (0, 0, 384, ("x", "y", "z")),
-    (0, 384, 256, ("y", "z", "x")),
+    (0, 384, 256, ("y", "x", "z")),
     (1, 640, 384, ("z", "y", "x")),
-    (1, 0, 256, ("x", "z", "y")),
+    (1, 0, 256, ("x", "y", "z")),
     (1, 256, 384, ("y", "x", "z")),
+)
+SCHEDULE = (
+    ("gather_first", 2), ("gather_first", 1), ("swap", 0), ("peak", 0), ("gather_second", 0), ("gather_second", 1),
+    ("gather_second", 2), ("partials", 0), ("peak", 1), ("ring_far", 0), ("gather_near", 1), ("ring_far", 3),
+    ("gather_near", 0), ("partials", 1), ("peak", 2), ("ring_near", 1), ("ring_near", 0), ("gather_near", 2),
+    ("ring_far", 1), ("ring_near", 4), ("ring_near", 3), ("gather_rest", 1), ("ring_far", 5), ("ring_near", 5),
+    ("ring_sum", 0), ("ring_far", 2), ("ring_sum", 1), ("gather_rest", 0), ("ring_sum", 3), ("ring_near", 2),
+    ("ring_sum", 2), ("ring_sum", 5), ("second_axis", 1), ("gather_far", 2), ("ring_far", 4), ("second_axis", 2),
+    ("second_axis", 0), ("second_axis", 3), ("gather_rest", 2), ("ring_sum", 4), ("third_axis", 2),
+    ("second_axis", 5), ("third_axis", 0), ("second_axis", 4), ("third_axis", 1), ("gather_far", 1),
+    ("third_axis", 3), ("third_axis", 5), ("gather_far", 0), ("third_axis", 4), ("matmuls", 0), ("peak", 3),
+    ("matmuls", 1), ("spread", 0), ("matmuls", 2), ("matmuls", 3), ("spread", 1), ("matmuls", 4), ("matmuls", 5),
+    ("matmuls", 6), ("spread_more", 0), ("matmuls", 7), ("spread_more", 1), ("spread_end", 1), ("keys", 0),
+    ("spread_end", 0), ("peak", 4),
 )
 GROUPS = len(REDUCE)
 HALF = ROWS // 2
@@ -72,12 +90,18 @@
             src_ref=src, dst_ref=dst, send_sem=send, recv_sem=recv, device_id=to, device_id_type=MESH
         )
 
-    sent = []
+    sent, landed = [], set()
 
     def start(copies):
         for copy in copies:
             copy.start()
             sent.append(copy)
+
+    def arrive(copies):
+        for copy in copies:
+            if id(copy) not in landed:
+                landed.add(id(copy))
+                copy.wait_recv()
 
     def hid_cols(slot, which):
         return pl.ds(pl.multiple_of((slot * 2 + which) * BLOCK, BLOCK), BLOCK)
@@ -101,14 +125,18 @@
     lim = jnp.full((1, WIDTH), limit[0], f32)
     scale = 448.0 / lim
 
-    def quantize(w, cols):
-        return jnp.clip(w.astype(f32) * scale[:, cols], -448.0, 448.0).astype(bf16)
-
-    split = GATHER[2][0]
-    for z in range(4):
-        codes[at["x"], at["y"], z, :, :split] = quantize(w_in[z * ROWS : (z + 1) * ROWS, :split], slice(0, split))
+    def quantize(w, first, size):
+        return jnp.clip(w.astype(f32) * scale[:, first : first + size], -448.0, 448.0).astype(bf16)
+
     own_rows = w_in[pl.ds(pl.multiple_of(at["z"] * ROWS, ROWS), ROWS), :]
-    codes[at["x"], at["y"], at["z"], :, split:] = quantize(own_rows[:, split:], slice(split, WIDTH))
+    for first, size, order in GATHER:
+        if order[0] == "z":
+            for z in range(4):
+                line = w_in[z * ROWS : (z + 1) * ROWS, first : first + size]
+                codes[at["x"], at["y"], z, :, first : first + size] = quantize(line, first, size)
+        else:
+            mine = own_rows[:, first : first + size]
+            codes[at["x"], at["y"], at["z"], :, first : first + size] = quantize(mine, first, size)
 
     pl.semaphore_wait(barrier, 10)
 
@@ -127,21 +155,20 @@
             for j in (1, 2, 3)
         ]
 
-    ag_first = gather_direct(2, 0)
-    start(ag_first)
-    ag_mid = [gather_direct(0, 1), gather_direct(1, 1), gather_direct(2, 1)]
-    start(ag_mid[0] + ag_mid[1])
+    ag_first = [[] if order[0] == "z" else gather_direct(k, 0) for k, (_, _, order) in enumerate(GATHER)]
+    ag_mid = [gather_direct(k, 1) for k in range(3)]
 
     swaps = [remote(cotangent, cot.at[1], swap_send.at[0], swap_recv.at[0], partner)]
     for s in range(SLOTS):
         swaps.append(
             remote(hidden.at[:, hid_cols(s, other)], hid.at[s, 1], swap_send.at[1 + s], swap_recv.at[1 + s], partner)
         )
-    start(swaps)
 
     peak[0] = jnp.max(
         jnp.abs(own_rows.astype(f32)).reshape(ROWS // 8, 8, WIDTH // 128, 128).max(axis=0), axis=1
     )
+
+    peaks = {}
 
     def peak_phase(p):
         targets = [partner] if p == 3 else [device(moved(at, AXES[p], j), core) for j in (1, 2, 3)]
@@ -150,20 +177,14 @@
             for j, to in enumerate(targets)
         ]
         start(copies)
-        return copies
-
-    def peak_join(p, copies):
+        peaks[p] = copies
+
+    def peak_join(p):
         best = peak[p]
-        for j, copy in enumerate(copies):
+        for j, copy in enumerate(peaks[p]):
             copy.wait_recv()
             best = jnp.maximum(best, peak_in[p, j])
         peak[p + 1] = best
-
-    peaks = peak_phase(0)
-
-    for copy in ag_first:
-        copy.wait_recv()
-    start(ag_mid[2])
 
     def partials(first, size, arrive):
         @pl.loop(0, SLOTS)
@@ -196,12 +217,6 @@
         for k in range(GROUPS)
     ]
 
-    def ring_begin(groups):
-        for k in groups:
-            start(rs_ring[k][0:2])
-        for k in groups:
-            start(rs_ring[k][2:4])
-
     def part(k, by, half, a, b):
         rows, first, size, order = REDUCE[k]
         where = {order[0]: lax.rem(at[order[0]] + by, 4), order[1]: 2 * half + a, order[2]: b}
@@ -219,7 +234,7 @@
 
     def ring_forward(k):
         for n, by, half in ((0, 1, 0), (1, 3, 1)):
-            rs_ring[k][n].wait_recv()
+            arrive([rs_ring[k][n]])
             add_landed(k, by, half, (n,))
             start([rs_ring[k][4 + n]])
 
@@ -241,16 +256,14 @@
     rs_third = [reduce_direct(k, 2) for k in range(GROUPS)]
 
     def ring_end(k):
-        for n in range(2, 6):
-            rs_ring[k][n].wait_recv()
+        arrive(rs_ring[k][2:])
         add_landed(k, 0, 0, (3, 4))
         add_landed(k, 0, 1, (2, 5))
         start(rs_second[k])
 
     def second_end(k):
         rows, first, size, order = REDUCE[k]
-        for copy in rs_second[k]:
-            copy.wait_recv()
+        arrive(rs_second[k])
 
         @pl.loop(0, 4)
         def _(b):
@@ -268,8 +281,7 @@
 
     def third_end(k):
         rows, first, size, order = REDUCE[k]
-        for copy in rs_third[k]:
-            copy.wait_recv()
+        arrive(rs_third[k])
         acc = partial[at["x"], at["y"], at["z"], half_rows(rows), pl.ds(first, size)].astype(f32)
         for j in range(3):
             acc += third_in[k][j].astype(f32)
@@ -293,9 +305,9 @@
         )
 
     def spread_more(half):
-        rep[half][0].wait_recv()
+        arrive(rep[half][:1])
         start(rep[half][4:6])
-        rep[half][3].wait_recv()
+        arrive(rep[half][3:4])
         start(rep[half][6:7])
 
     def gather_ring(k, n, by, half):
@@ -313,89 +325,109 @@
         for k in range(3)
     ]
 
-    def gather_last(k):
-        for copy in ag_mid[k]:
-            copy.wait_recv()
-        start(ag_ring[k][:4])
-
-    def gather_forward(k):
+    def gather_near(k):
+        arrive(ag_mid[k])
+        start(ag_ring[k][:2])
+
+    def gather_far(k):
         for n in (0, 1):
-            ag_ring[k][n].wait_recv()
+            arrive([ag_ring[k][n]])
             start([ag_ring[k][4 + n]])
 
     unscale = limit[0] * (1.0 / 448.0)
 
-    def matmuls(lo, hi):
-        @pl.loop(lo, hi)
-        def _(s):
-            w_s = codes[s // 2, pl.ds(lax.rem(s, 2) * 2, 2)].reshape(BLOCK, WIDTH)
-            h = hid[s].reshape(2 * TOK, BLOCK)
-            for n in range(0, WIDTH, 512):
-                keys_acc[:, n : n + 512] += jnp.dot(h, w_s[:, n : n + 512], preferred_element_type=f32)
-            c_all = cot[...].reshape(2 * TOK, WIDTH)
-            for n in range(0, BLOCK, 256):
-                g = lax.dot_general(c_all, w_s[n : n + 256], (((1,), (1,)), ((), ())), preferred_element_type=f32)
-                g = (g * unscale).astype(bf16)
-                grad_stage[s, :, n : n + 256] = g[TOK:]
-                grad_out[:, pl.ds(pl.multiple_of((s * 2 + core) * BLOCK + n, 256), 256)] = g[:TOK]
-            remote(
-                grad_stage.at[s], grad_out.at[:, hid_cols(s, core)], grad_send.at[s], grad_recv.at[s], partner
-            ).start()
-
-    load_c.wait()
-    swaps[0].wait_recv()
-    partials(512, 512, True)
-    ring_begin((0, 3))
-    partials(0, 512, False)
-    ring_begin((1, 2))
-    ring_begin((4, 5))
-    peak_join(0, peaks)
-    peaks = peak_phase(1)
-    for k in range(3):
-        gather_last(k)
-    keys_acc[...] = jnp.zeros_like(keys_acc)
-    for k in range(GROUPS):
-        ring_forward(k)
-    peak_join(1, peaks)
-    peaks = peak_phase(2)
-    for k in range(3):
-        gather_forward(k)
-    for k in range(GROUPS):
-        ring_end(k)
-    peak_join(2, peaks)
-    peaks = peak_phase(3)
-    for k in range(3):
-        for copy in ag_ring[k][2:]:
-            copy.wait_recv()
-    matmuls(0, 2)
-    for k in (0, 1, 2):
-        second_end(k)
-    matmuls(2, 4)
-    for k in (3, 4, 5):
-        second_end(k)
-    matmuls(4, 6)
-    for k in (0, 1, 2):
-        third_end(k)
-    start(rep[0][:4])
-    matmuls(6, 8)
-    for k in (3, 4, 5):
-        third_end(k)
-    start(rep[1][:4])
-    keys_send[...] = keys_acc[TOK:].astype(bf16)
+    last = {order[2]: k for k, (_, _, order) in enumerate(GATHER)}
+
+    def matmuls(n):
+        if n == 0:
+            for k in range(3):
+                arrive(ag_ring[k][:4])
+            arrive(ag_ring[last["z"]][4:])
+        elif n == 3:
+            arrive(ag_ring[last["y"]][4:])
+        elif n == 6:
+            arrive(ag_ring[last["x"]][4:])
+        by, across = ((0, 0), (1, 0), (3, 0), (0, 1), (1, 1), (3, 1), (2, 0), (2, 1))[n]
+        x = lax.rem(at["x"] + by, 4)
+        y_hi = lax.rem(at["y"] // 2 + across, 2)
+        s = x * 2 + y_hi
+        w_s = codes[x, pl.ds(y_hi * 2, 2)].reshape(BLOCK, WIDTH)
+        h = hid[s].reshape(2 * TOK, BLOCK)
+        for c in range(0, WIDTH, 512):
+            term = jnp.dot(h, w_s[:, c : c + 512], preferred_element_type=f32)
+            keys_acc[:, c : c + 512] = term if n == 0 else keys_acc[:, c : c + 512] + term
+        c_all = cot[...].reshape(2 * TOK, WIDTH)
+        for c in range(0, BLOCK, 256):
+            g = lax.dot_general(c_all, w_s[c : c + 256], (((1,), (1,)), ((), ())), preferred_element_type=f32)
+            g = (g * unscale).astype(bf16)
+            grad_stage[s, :, c : c + 256] = g[TOK:]
+            grad_out[:, pl.ds(pl.multiple_of((s * 2 + core) * BLOCK + c, 256), 256)] = g[:TOK]
+        remote(
+            grad_stage.at[s], grad_out.at[:, hid_cols(s, core)], grad_send.at[s], grad_recv.at[s], partner
+        ).start()
+        if n == SLOTS - 1:
+            keys_send[...] = keys_acc[TOK:].astype(bf16)
+            start([key_copy])
+
     key_copy = remote(keys_send, keys_recv, key_send.at[0], key_recv.at[0], partner)
-    start([key_copy])
-    spread_more(0)
-    peak_join(3, peaks)
-    ratio_out[0] = jnp.max(peak[4] / jnp.full((8, 128), limit[0], f32))
-    key_copy.wait_recv()
-    keys_out[...] = ((keys_acc[:TOK] + keys_recv[...].astype(f32)) * unscale).astype(bf16)
-    spread_more(1)
+
+    def step(name, n):
+        if name == "gather_first":
+            start(ag_first[n])
+        elif name == "gather_second":
+            arrive(ag_first[n])
+            start(ag_mid[n])
+        elif name == "gather_near":
+            gather_near(n)
+        elif name == "gather_rest":
+            start(ag_ring[n][2:4])
+        elif name == "gather_far":
+            gather_far(n)
+        elif name == "swap":
+            start(swaps)
+        elif name == "partials":
+            if n == 0:
+                load_c.wait()
+                arrive(swaps[:1])
+            partials(512 - 512 * n, 512, n == 0)
+        elif name == "ring_far":
+            start(rs_ring[n][:2])
+        elif name == "ring_near":
+            start(rs_ring[n][2:4])
+        elif name == "ring_sum":
+            ring_forward(n)
+        elif name == "second_axis":
+            ring_end(n)
+        elif name == "third_axis":
+            second_end(n)
+        elif name == "spread":
+            for k in range(3 * n, 3 * n + 3):
+                third_end(k)
+            start(rep[n][:4])
+        elif name == "spread_more":
+            spread_more(n)
+        elif name == "spread_end":
+            arrive(rep[n])
+        elif name == "matmuls":
+            matmuls(n)
+        elif name == "keys":
+            arrive([key_copy])
+            keys_out[...] = ((keys_acc[:TOK] + keys_recv[...].astype(f32)) * unscale).astype(bf16)
+        elif name == "peak":
+            if n > 0:
+                peak_join(n - 1)
+            if n < 4:
+                peak_phase(n)
+            else:
+                ratio_out[0] = jnp.max(peak[4] / jnp.full((8, 128), limit[0], f32))
+        else:
+            raise ValueError(name)
+
+    for name, n in SCHEDULE:
+        step(name, n)
 
     for s in range(SLOTS):
         remote(grad_stage.at[s], grad_out.at[:, hid_cols(s, core)], grad_send.at[s], grad_recv.at[s], partner).wait()
-    for half in (0, 1):
-        for n in (1, 2, 4, 5, 6):
-            rep[half][n].wait_recv()
     for copy in sent:
         copy.wait_send()
 

time: 99.3 us -> 94.8 us (0.955)
  Pallas kernels: 95.3 us -> 91.6 us
    pallas_call x1, Pallas kernels: 92.8 us -> 89.1 us  [body(): pl.pallas_call(kernel, out_shape=(*[pltpu.VMEM(shape, bf16) for shape in...]
where the time goes in v3:
time: 94.8 us; the launch traced here: 94.7 us
  Pallas kernels  91.6 us (97%)
  between operations  3.05 us (3%)
    pallas_call x1, Pallas kernels, body(): pl.pallas_call(kernel, out_shape=(*[pltpu.VMEM(shape, bf16) for shape in...  89.1 us
    pallas_call x1, Pallas kernels, body(): pl.pallas_call(place, out_shape=tuple((jax.ShapeDtypeStruct(shape, bf16)...  2.52 us

profile of v3, /device:TPU:0, one launch (start us, length us, event | category | flops | bytes accessed | tf_op | source)
XLA Modules:
  0.0 94.7 jit_solution(2694697153243123358)
XLA Ops:
  1.3 89.1 %shard_map.75 = (bf16[256,1024]{1,0:T(8,128)(2,1)S(1)}, bf16[256,8192]{1,0:T(8,128)(2,1)S(1)}, bf16[512,1024]{1,0:T(8,128)(2,1)S(1)}, f32[1]{0:T(128)}) custom-call(bf16[256,8192]{1,0:T(8,128)(2,1)} %hidden.1, bf16[512,1024]{1,0:T(8,128)(2,1)} %weight.1, f32[1]{0:T(128)S(6)} %copy.9.limit, bf16[256,1024]{1,0:T(8,128)(2,1)} %cotangent.1), custom_call_target="tpu_custom_call" | custom-call | tf_op jit(solution)/shard_map/pallas_call | solution.py:460
  90.4 2.5 %shard_map.76 = (bf16[256,1024]{1,0:T(8,128)(2,1)}, bf16[256,8192]{1,0:T(8,128)(2,1)}, bf16[512,1024]{1,0:T(8,128)(2,1)}) custom-call(bf16[256,1024]{1,0:T(8,128)(2,1)S(1)} %get-tuple-element.11.keys, bf16[256,8192]{1,0:T(8,128)(2,1)S(1)} %get-tuple-element.12.grad, bf16[512,1024]{1,0:T(8,128)(2,1)S(1)} %get-tuple-element.13.wgrad), custom_call_target="tpu_custom_call" | custom-call | tf_op jit(solution)/shard_map/pallas_call | solution.py:503

commit v4 on v3

--- a/solution.py
+++ b/solution.py
@@ -14,33 +14,33 @@
 BLOCK = 512
 GATHER = (
     (0, 384, ("z", "y", "x")),
-    (384, 256, ("x", "z", "y")),
-    (640, 384, ("y", "x", "z")),
+    (384, 384, ("z", "x", "y")),
+    (768, 256, ("x", "y", "z")),
 )
 REDUCE = (
-    (0, 640, 384, ("z", "y", "x")),
-    (0, 0, 384, ("x", "y", "z")),
-    (0, 384, 256, ("y", "x", "z")),
-    (1, 640, 384, ("z", "y", "x")),
-    (1, 0, 256, ("x", "y", "z")),
-    (1, 256, 384, ("y", "x", "z")),
+    (0, 0, 384, ("z", "x", "y")),
+    (0, 384, 256, ("x", "y", "z")),
+    (0, 640, 384, ("y", "z", "x")),
+    (1, 0, 384, ("z", "x", "y")),
+    (1, 384, 384, ("x", "z", "y")),
+    (1, 768, 256, ("y", "z", "x")),
 )
 SCHEDULE = (
-    ("gather_first", 2), ("gather_first", 1), ("swap", 0), ("peak", 0), ("gather_second", 0), ("gather_second", 1),
-    ("gather_second", 2), ("partials", 0), ("peak", 1), ("ring_far", 0), ("gather_near", 1), ("ring_far", 3),
-    ("gather_near", 0), ("partials", 1), ("peak", 2), ("ring_near", 1), ("ring_near", 0), ("gather_near", 2),
-    ("ring_far", 1), ("ring_near", 4), ("ring_near", 3), ("gather_rest", 1), ("ring_far", 5), ("ring_near", 5),
-    ("ring_sum", 0), ("ring_far", 2), ("ring_sum", 1), ("gather_rest", 0), ("ring_sum", 3), ("ring_near", 2),
-    ("ring_sum", 2), ("ring_sum", 5), ("second_axis", 1), ("gather_far", 2), ("ring_far", 4), ("second_axis", 2),
-    ("second_axis", 0), ("second_axis", 3), ("gather_rest", 2), ("ring_sum", 4), ("third_axis", 2),
-    ("second_axis", 5), ("third_axis", 0), ("second_axis", 4), ("third_axis", 1), ("gather_far", 1),
-    ("third_axis", 3), ("third_axis", 5), ("gather_far", 0), ("third_axis", 4), ("matmuls", 0), ("peak", 3),
-    ("matmuls", 1), ("spread", 0), ("matmuls", 2), ("matmuls", 3), ("spread", 1), ("matmuls", 4), ("matmuls", 5),
-    ("matmuls", 6), ("spread_more", 0), ("matmuls", 7), ("spread_more", 1), ("spread_end", 1), ("keys", 0),
-    ("spread_end", 0), ("peak", 4),
+    ("gather_second", 0), ("gather_second", 1), ("gather_first", 2), ("swap", 0), ("peak", 0), ("partials", 0),
+    ("peak", 1), ("ring_far", 0), ("ring_far", 3), ("ring_far", 1), ("ring_far", 2), ("ring_far", 4),
+    ("ring_far", 5), ("ring_sum", 1), ("ring_near", 0), ("gather_second", 2), ("ring_sum", 5), ("peak", 2),
+    ("gather_near", 0), ("gather_second_far", 1), ("ring_sum", 3), ("ring_near", 5), ("ring_near", 1),
+    ("ring_sum", 2), ("ring_near", 2), ("ring_near", 3), ("ring_sum", 0), ("gather_second_far", 2),
+    ("second_axis", 5), ("ring_near", 4), ("gather_near", 1), ("second_axis", 2), ("second_axis", 1),
+    ("ring_sum", 4), ("second_axis", 0), ("second_axis", 3), ("gather_near", 2), ("gather_rest", 1),
+    ("third_axis", 5), ("gather_rest", 0), ("gather_rest", 2), ("third_axis", 2), ("third_axis", 0),
+    ("gather_far", 2), ("second_axis", 4), ("gather_far", 0), ("gather_far", 1), ("third_axis", 3), ("matmuls", 0),
+    ("peak", 3), ("third_axis", 1), ("matmuls", 1), ("matmuls", 2), ("third_axis", 4), ("spread", 0), ("matmuls", 3),
+    ("matmuls", 4), ("spread", 1), ("matmuls", 5), ("matmuls", 6), ("spread_more", 0), ("matmuls", 7),
+    ("spread_more", 1), ("keys", 0), ("spread_end", 1), ("spread_end", 0), ("peak", 4),
 )
 GROUPS = len(REDUCE)
-HALF = ROWS // 2
+PARTS = ((0, 32), (32, 32))
 
 
 def position():
@@ -69,15 +69,15 @@
 
 
 def half_rows(half):
-    return pl.ds(half * HALF, HALF)
+    return pl.ds(*PARTS[half])
 
 
 def kernel(hidden, weight, limit, cotangent, keys_out, grad_out, wgrad_out, ratio_out, *scratch):
-    (w_in, codes, partial, hid, cot, keys_acc, keys_send, keys_recv, grad_stage, peak, peak_in) = scratch[:11]
-    landings = scratch[11 : 11 + 3 * GROUPS]
+    (ratio, w_in, codes, partial, hid, cot, keys_acc, keys_send, keys_recv, grad_stage, peak, peak_in) = scratch[:12]
+    landings = scratch[12 : 12 + 3 * GROUPS]
     first_in, second_in, third_in = (landings[n * GROUPS : (n + 1) * GROUPS] for n in range(3))
     (load_sem, swap_send, swap_recv, ag_send, ag_recv, rs_send, rs_recv, rep_send, rep_recv,
-     peak_send, peak_recv, key_send, key_recv, grad_send, grad_recv) = scratch[11 + 3 * GROUPS :]
+     peak_send, peak_recv, key_send, key_recv, grad_send, grad_recv) = scratch[12 + 3 * GROUPS :]
 
     at, core = position()
     other = 1 - core
@@ -106,9 +106,7 @@
     def hid_cols(slot, which):
         return pl.ds(pl.multiple_of((slot * 2 + which) * BLOCK, BLOCK), BLOCK)
 
-    load_w = pltpu.make_async_copy(
-        weight.at[pl.ds(pl.multiple_of(y_lo * 4 * ROWS, 4 * ROWS), 4 * ROWS)], w_in, load_sem.at[0]
-    )
+    load_w = pltpu.make_async_copy(weight, w_in, load_sem.at[0])
     load_w.start()
     load_c = pltpu.make_async_copy(cotangent, cot.at[0], load_sem.at[1])
     load_c.start()
@@ -128,35 +126,60 @@
     def quantize(w, first, size):
         return jnp.clip(w.astype(f32) * scale[:, first : first + size], -448.0, 448.0).astype(bf16)
 
-    own_rows = w_in[pl.ds(pl.multiple_of(at["z"] * ROWS, ROWS), ROWS), :]
+    def rows_of(lo, z):
+        return pl.ds(pl.multiple_of((lo * 4 + z) * ROWS, ROWS), ROWS)
+
+    own_rows = w_in[rows_of(y_lo, at["z"]), :]
+    pair = at["y"] - y_lo
     for first, size, order in GATHER:
-        if order[0] == "z":
+        cols = slice(first, first + size)
+        if order[:2] == ("z", "y"):
+            block = quantize(w_in[:, cols], first, size)
+            codes[at["x"], pl.ds(pair, 2), :, :, cols] = block.reshape(2, 4, ROWS, size)
+        elif order[0] == "z":
             for z in range(4):
-                line = w_in[z * ROWS : (z + 1) * ROWS, first : first + size]
-                codes[at["x"], at["y"], z, :, first : first + size] = quantize(line, first, size)
+                codes[at["x"], at["y"], z, :, cols] = quantize(w_in[rows_of(y_lo, z), cols], first, size)
         else:
-            mine = own_rows[:, first : first + size]
-            codes[at["x"], at["y"], at["z"], :, first : first + size] = quantize(mine, first, size)
+            codes[at["x"], at["y"], at["z"], :, cols] = quantize(own_rows[:, cols], first, size)
 
     pl.semaphore_wait(barrier, 10)
 
     def view(ref, where, rows, cols):
         return ref.at[where["x"], where["y"], where["z"], rows, cols]
 
-    def gather_direct(k, phase):
+    def gather_direct(k):
         first, size, order = GATHER[k]
-        where = dict(at)
-        for axis in order[:phase]:
-            where[axis] = whole()
-        src = view(codes, where, slice(None), pl.ds(first, size))
+        src = view(codes, at, slice(None), pl.ds(first, size))
         return [
-            remote(src, src, ag_send.at[k, phase * 3 + j - 1], ag_recv.at[k, phase * 3 + j - 1],
-                   device(moved(at, order[phase], j), core))
+            remote(src, src, ag_send.at[k, j - 1], ag_recv.at[k, j - 1], device(moved(at, order[0], j), core))
             for j in (1, 2, 3)
         ]
 
-    ag_first = [[] if order[0] == "z" else gather_direct(k, 0) for k, (_, _, order) in enumerate(GATHER)]
-    ag_mid = [gather_direct(k, 1) for k in range(3)]
+    def gather_ring(k, phase, n, by, half):
+        first, size, order = GATHER[k]
+        where = {order[0]: pl.ds(2 * half, 2), order[1]: whole(), order[2]: at[order[2]]}
+        where[order[phase]] = lax.rem(at[order[phase]] + by, 4)
+        src = view(codes, where, slice(None), pl.ds(first, size))
+        to = device(moved(at, order[phase], 1 if n % 2 == 0 else 3), core)
+        m = 3 + 6 * (phase - 1) + n
+        return remote(src, src, ag_send.at[k, m], ag_recv.at[k, m], to)
+
+    def gather_both_ways(k, phase):
+        steps = ((0, 0), (0, 1), (0, 1), (0, 0), (3, 0), (1, 1))
+        return [gather_ring(k, phase, n, by, half) for n, (by, half) in enumerate(steps)]
+
+    def gather_across(k):
+        first, size, order = GATHER[k]
+        src = view(codes, {**at, "y": pl.ds(pair, 2), "z": whole()}, slice(None), pl.ds(first, size))
+        to = device({**at, "y": lax.rem(at["y"] + 3 - 2 * y_lo, 4)}, core)
+        return [remote(src, src, ag_send.at[k, 3], ag_recv.at[k, 3], to)]
+
+    ag_first = [[] if order[0] == "z" else gather_direct(k) for k, (_, _, order) in enumerate(GATHER)]
+    ag_mid = [
+        gather_across(k) if order[:2] == ("z", "y") else gather_both_ways(k, 1)
+        for k, (_, _, order) in enumerate(GATHER)
+    ]
+    ag_ring = [gather_both_ways(k, 2) for k in range(3)]
 
     swaps = [remote(cotangent, cot.at[1], swap_send.at[0], swap_recv.at[0], partner)]
     for s in range(SLOTS):
@@ -186,21 +209,18 @@
             best = jnp.maximum(best, peak_in[p, j])
         peak[p + 1] = best
 
-    def partials(first, size, arrive):
+    def partials():
         @pl.loop(0, SLOTS)
         def _(s):
-            if arrive:
-                pltpu.make_async_copy(hidden.at[:, hid_cols(0, core)], hid.at[s, 0], load_sem.at[2 + s]).wait()
-                remote(
-                    hidden.at[:, hid_cols(0, other)], hid.at[s, 1], swap_send.at[1 + s], swap_recv.at[1 + s], partner
-                ).wait_recv()
+            pltpu.make_async_copy(hidden.at[:, hid_cols(0, core)], hid.at[s, 0], load_sem.at[2 + s]).wait()
+            remote(
+                hidden.at[:, hid_cols(0, other)], hid.at[s, 1], swap_send.at[1 + s], swap_recv.at[1 + s], partner
+            ).wait_recv()
             term = lax.dot_general(
-                hid[s].reshape(2 * TOK, BLOCK), cot[:, :, first : first + size].reshape(2 * TOK, size),
+                hid[s].reshape(2 * TOK, BLOCK), cot[...].reshape(2 * TOK, WIDTH),
                 (((0,), (0,)), ((), ())), preferred_element_type=f32,
             )
-            partial[s // 2, pl.ds(lax.rem(s, 2) * 2, 2), :, :, first : first + size] = term.astype(bf16).reshape(
-                2, 4, ROWS, size
-            )
+            partial[s // 2, pl.ds(lax.rem(s, 2) * 2, 2)] = term.astype(bf16).reshape(2, 4, ROWS, WIDTH)
 
     def ring(k, n, by, half, slot):
         rows, first, size, order = REDUCE[k]
@@ -277,7 +297,8 @@
         start(rs_third[k])
 
     def piece(half, lo, z):
-        return pl.ds(pl.multiple_of((lo * 4 + z) * ROWS + half * HALF, HALF), HALF)
+        row, rows = PARTS[half]
+        return pl.ds(pl.multiple_of((lo * 4 + z) * ROWS + row, 16), rows)
 
     def third_end(k):
         rows, first, size, order = REDUCE[k]
@@ -310,29 +331,14 @@
         arrive(rep[half][3:4])
         start(rep[half][6:7])
 
-    def gather_ring(k, n, by, half):
-        first, size, order = GATHER[k]
-        where = {axis: whole() for axis in AXES}
-        where[order[2]] = lax.rem(at[order[2]] + by, 4)
-        where[order[0]] = pl.ds(2 * half, 2)
-        src = view(codes, where, slice(None), pl.ds(first, size))
-        to = device(moved(at, order[2], 1 if n % 2 == 0 else 3), core)
-        return remote(src, src, ag_send.at[k, 6 + n], ag_recv.at[k, 6 + n], to)
-
-    ag_ring = [
-        [gather_ring(k, 0, 0, 0), gather_ring(k, 1, 0, 1), gather_ring(k, 2, 0, 1), gather_ring(k, 3, 0, 0),
-         gather_ring(k, 4, 3, 0), gather_ring(k, 5, 1, 1)]
-        for k in range(3)
-    ]
+    def gather_pass(copies):
+        for n in (0, 1):
+            arrive([copies[n]])
+            start([copies[4 + n]])
 
     def gather_near(k):
         arrive(ag_mid[k])
         start(ag_ring[k][:2])
-
-    def gather_far(k):
-        for n in (0, 1):
-            arrive([ag_ring[k][n]])
-            start([ag_ring[k][4 + n]])
 
     unscale = limit[0] * (1.0 / 448.0)
 
@@ -369,6 +375,7 @@
             keys_send[...] = keys_acc[TOK:].astype(bf16)
             start([key_copy])
 
+    place_ratio = pltpu.make_async_copy(ratio, ratio_out, load_sem.at[2 + SLOTS])
     key_copy = remote(keys_send, keys_recv, key_send.at[0], key_recv.at[0], partner)
 
     def step(name, n):
@@ -376,20 +383,22 @@
             start(ag_first[n])
         elif name == "gather_second":
             arrive(ag_first[n])
-            start(ag_mid[n])
+            start(ag_mid[n][:4])
+        elif name == "gather_second_far":
+            if len(ag_mid[n]) > 1:
+                gather_pass(ag_mid[n])
         elif name == "gather_near":
             gather_near(n)
         elif name == "gather_rest":
             start(ag_ring[n][2:4])
         elif name == "gather_far":
-            gather_far(n)
+            gather_pass(ag_ring[n])
         elif name == "swap":
             start(swaps)
         elif name == "partials":
-            if n == 0:
-                load_c.wait()
-                arrive(swaps[:1])
-            partials(512 - 512 * n, 512, n == 0)
+            load_c.wait()
+            arrive(swaps[:1])
+            partials()
         elif name == "ring_far":
             start(rs_ring[n][:2])
         elif name == "ring_near":
@@ -419,23 +428,25 @@
             if n < 4:
                 peak_phase(n)
             else:
-                ratio_out[0] = jnp.max(peak[4] / jnp.full((8, 128), limit[0], f32))
+                ratio[0] = jnp.max(peak[4] / jnp.full((8, 128), limit[0], f32))
+                place_ratio.start()
         else:
             raise ValueError(name)
 
     for name, n in SCHEDULE:
         step(name, n)
 
+    place_ratio.wait()
     for s in range(SLOTS):
         remote(grad_stage.at[s], grad_out.at[:, hid_cols(s, core)], grad_send.at[s], grad_recv.at[s], partner).wait()
     for copy in sent:
         copy.wait_send()
 
 
-def place(keys, grad, wgrad, keys_out, grad_out, wgrad_out, sem):
+def place(keys, grad, wgrad, ratio, keys_out, grad_out, wgrad_out, ratio_out, sem):
     copies = [
         pltpu.make_async_copy(src, dst, sem.at[n])
-        for n, (src, dst) in enumerate(((grad, grad_out), (wgrad, wgrad_out), (keys, keys_out)))
+        for n, (src, dst) in enumerate(((grad, grad_out), (wgrad, wgrad_out), (keys, keys_out), (ratio, ratio_out)))
     ]
     for copy in copies:
         copy.start()
@@ -444,9 +455,9 @@
 
 
 def landing(k, phase):
-    size = REDUCE[k][2]
+    half, _, size, _ = REDUCE[k]
     shape = (spot(k, 6, 2, 4), (3, 4), (3,))[phase]
-    return pltpu.VMEM((*shape, HALF, size), jnp.bfloat16)
+    return pltpu.VMEM((*shape, PARTS[half][1], size), jnp.bfloat16)
 
 
 def body(hidden_states, key_weight, previous_peak, key_cotangent):
@@ -461,9 +472,10 @@
         kernel,
         out_shape=(*[pltpu.VMEM(shape, bf16) for shape in shapes], jax.ShapeDtypeStruct((1,), f32)),
         in_specs=[hbm, hbm, smem, hbm],
-        out_specs=(vmem, vmem, vmem, smem),
+        out_specs=(vmem, vmem, vmem, any_space),
         scratch_shapes=[
-            pltpu.VMEM((4 * ROWS, WIDTH), bf16),
+            pltpu.SMEM((1,), f32),
+            pltpu.VMEM((BLOCK, WIDTH), bf16),
             pltpu.VMEM((4, 4, 4, ROWS, WIDTH), bf16),
             pltpu.VMEM((4, 4, 4, ROWS, WIDTH), bf16),
             pltpu.VMEM((SLOTS, 2, TOK, BLOCK), bf16),
@@ -475,11 +487,11 @@
             pltpu.VMEM((5, 8, 128), f32),
             pltpu.VMEM((4, 3, 8, 128), f32),
             *[landing(k, phase) for phase in range(3) for k in range(GROUPS)],
-            dma((2 + SLOTS,)),
+            dma((3 + SLOTS,)),
             dma((1 + SLOTS,)),
             dma((1 + SLOTS,)),
-            dma((3, 12)),
-            dma((3, 12)),
+            dma((3, 15)),
+            dma((3, 15)),
             dma((GROUPS, 12)),
             dma((GROUPS, 12)),
             dma((2, 7)),
@@ -500,15 +512,14 @@
         previous_peak,
         pltpu.with_memory_space_constraint(key_cotangent, pltpu.HBM),
     )
-    keys, grad, wgrad = pl.pallas_call(
+    return pl.pallas_call(
         place,
-        out_shape=tuple(jax.ShapeDtypeStruct(shape, bf16) for shape in shapes),
-        in_specs=[any_space] * 3,
-        out_specs=(any_space,) * 3,
-        scratch_shapes=[dma((3,))],
+        out_shape=(*[jax.ShapeDtypeStruct(shape, bf16) for shape in shapes], jax.ShapeDtypeStruct((1,), f32)),
+        in_specs=[any_space] * 4,
+        out_specs=(any_space,) * 4,
+        scratch_shapes=[dma((4,))],
         compiler_params=pltpu.CompilerParams(vmem_limit_bytes=2**20),
-    )(*[pltpu.with_memory_space_constraint(array, pltpu.VMEM) for array in results])
-    return keys, grad, wgrad, ratio
+    )(*[pltpu.with_memory_space_constraint(array, pltpu.VMEM) for array in results], ratio)
 
 
 def solution(mesh):

time: 94.8 us -> 92.5 us (0.976)
  between operations: 3.05 us -> 1.29 us
    pallas_call x1, Pallas kernels: 89.1 us -> 88 us  [body(): pl.pallas_call(kernel, out_shape=(*[pltpu.VMEM(shape, bf16) for shape in...]
where the time goes in v4:
time: 92.5 us; the launch traced here: 92.4 us
  Pallas kernels  91.1 us (98%)
  between operations  1.29 us (1%)
    pallas_call x1, Pallas kernels, body(): pl.pallas_call(kernel, out_shape=(*[pltpu.VMEM(shape, bf16) for shape in...  88 us
    pallas_call x1, Pallas kernels, body(): pl.pallas_call(place, out_shape=(*[jax.ShapeDtypeStruct(shape, bf16) for...  3.08 us

profile of v4, /device:TPU:0, one launch (start us, length us, event | category | flops | bytes accessed | tf_op | source)
XLA Modules:
  0.0 92.4 jit_solution(571204109212689008)
XLA Ops:
  1.3 88.0 %shard_map.75 = (bf16[256,1024]{1,0:T(8,128)(2,1)S(1)}, bf16[256,8192]{1,0:T(8,128)(2,1)S(1)}, bf16[512,1024]{1,0:T(8,128)(2,1)S(1)}, f32[1]{0:T(128)}) custom-call(bf16[256,8192]{1,0:T(8,128)(2,1)} %hidden.1, bf16[512,1024]{1,0:T(8,128)(2,1)} %weight.1, f32[1]{0:T(128)S(6)} %copy.8.limit, bf16[256,1024]{1,0:T(8,128)(2,1)} %cotangent.1), custom_call_target="tpu_custom_call" | custom-call | tf_op jit(solution)/shard_map/pallas_call | solution.py:471
  89.3 3.1 %shard_map.76 = (bf16[256,1024]{1,0:T(8,128)(2,1)}, bf16[256,8192]{1,0:T(8,128)(2,1)}, bf16[512,1024]{1,0:T(8,128)(2,1)}, f32[1]{0:T(128)}) custom-call(bf16[256,1024]{1,0:T(8,128)(2,1)S(1)} %get-tuple-element.8.keys, bf16[256,8192]{1,0:T(8,128)(2,1)S(1)} %get-tuple-element.9.grad, bf16[512,1024]{1,0:T(8,128)(2,1)S(1)} %get-tuple-element.10.wgrad, ...), custom_call_target="tpu_custom_call" | custom-call | tf_op jit(solution)/shard_map/pallas_call | solution.py:515

commit v5 on v4

--- a/solution.py
+++ b/solution.py
@@ -421,6 +421,7 @@
             matmuls(n)
         elif name == "keys":
             arrive([key_copy])
+            leave()
             keys_out[...] = ((keys_acc[:TOK] + keys_recv[...].astype(f32)) * unscale).astype(bf16)
         elif name == "peak":
             if n > 0:
@@ -433,12 +434,21 @@
         else:
             raise ValueError(name)
 
+    def leave():
+        for s in range(SLOTS):
+            remote(
+                grad_stage.at[s], grad_out.at[:, hid_cols(s, core)], grad_send.at[s], grad_recv.at[s], partner
+            ).wait()
+        last = {id(copy) for half in (0, 1) for copy in rep[half]}
+        for copy in sent:
+            if id(copy) not in last:
+                copy.wait_send()
+        sent[:] = [copy for copy in sent if id(copy) in last]
+
     for name, n in SCHEDULE:
         step(name, n)
 
     place_ratio.wait()
-    for s in range(SLOTS):
-        remote(grad_stage.at[s], grad_out.at[:, hid_cols(s, core)], grad_send.at[s], grad_recv.at[s], partner).wait()
     for copy in sent:
         copy.wait_send()
 

time: 92.5 us -> 92.3 us (level)
  no operation moved by 1% of the time
where the time goes in v5:
time: 92.3 us; the launch traced here: 92.2 us
  Pallas kernels  90.9 us (98%)
  between operations  1.29 us (1%)
    pallas_call x1, Pallas kernels, body(): pl.pallas_call(kernel, out_shape=(*[pltpu.VMEM(shape, bf16) for shape in...  87.8 us
    pallas_call x1, Pallas kernels, body(): pl.pallas_call(place, out_shape=(*[jax.ShapeDtypeStruct(shape, bf16) for...  3.08 us

profile of v5, /device:TPU:0, one launch (start us, length us, event | category | flops | bytes accessed | tf_op | source)
XLA Modules:
  0.0 92.2 jit_solution(14865901211039906366)
XLA Ops:
  1.3 87.8 %shard_map.75 = (bf16[256,1024]{1,0:T(8,128)(2,1)S(1)}, bf16[256,8192]{1,0:T(8,128)(2,1)S(1)}, bf16[512,1024]{1,0:T(8,128)(2,1)S(1)}, f32[1]{0:T(128)}) custom-call(bf16[256,8192]{1,0:T(8,128)(2,1)} %hidden.1, bf16[512,1024]{1,0:T(8,128)(2,1)} %weight.1, f32[1]{0:T(128)S(6)} %copy.8.limit, bf16[256,1024]{1,0:T(8,128)(2,1)} %cotangent.1), custom_call_target="tpu_custom_call" | custom-call | tf_op jit(solution)/shard_map/pallas_call | solution.py:481
  89.1 3.1 %shard_map.76 = (bf16[256,1024]{1,0:T(8,128)(2,1)}, bf16[256,8192]{1,0:T(8,128)(2,1)}, bf16[512,1024]{1,0:T(8,128)(2,1)}, f32[1]{0:T(128)}) custom-call(bf16[256,1024]{1,0:T(8,128)(2,1)S(1)} %get-tuple-element.8.keys, bf16[256,8192]{1,0:T(8,128)(2,1)S(1)} %get-tuple-element.9.grad, bf16[512,1024]{1,0:T(8,128)(2,1)S(1)} %get-tuple-element.10.wgrad, ...), custom_call_target="tpu_custom_call" | custom-call | tf_op jit(solution)/shard_map/pallas_call | solution.py:525
